TPU v7x, 32 devices: a whole 2x2x4 slice. The times are simulated.
32 devices in a mesh: row: 2 (over y), col: 16 (over z, x, core).
Axes of the slice: x: 2, y: 2, z: 4, core: 2. Of those that a mesh axis runs over, the one named last changes fastest.
Arguments:
- points: float32 [16, 4096], P(None, ('row', 'col')), may hold values from -6 to 6
- inverse_length: float32 [16], replicated, may hold values from 0.35 to 1.4
- target: float32 [4096], P(('row', 'col')), may hold values from -6 to 6
- probe_bits: int32 [15, 4096], P(None, ('row', 'col')), may hold values from 0 to 1
- leaf_inverse: float32 [4096, 128], P(('row', 'col')), may hold values from -1 to 4, as said below
- top_basis: float32 [64, 4096], P(None, ('row', 'col')), may hold values from -0.25 to 0.25
- sub_basis: float32 [64, 4096], P(None, ('row', 'col')), may hold values from -0.25 to 0.25
Outputs:
- solution: float32 [16, 4096], P(None, ('row', 'col'))
- residual: float32 [16, 4096], P(None, ('row', 'col'))
- coefficients: float32 [2, 2, 16], replicated
Inputs may be any that keep to these rules, and one draw needn't show every extreme that they name: `leaf_inverse`: each leaf block is symmetric, and each of its diagonal entries exceeds the sum of the absolute values of the other entries of its row.
All inputs are finite; a program needn't handle non-finite values.
Results may differ from a plain program's by a relative error of at most 0.0003.
Values sent between devices are 32-bit elements; how exact they have to be, the bound alone decides.
A program may use at most 64 MiB of HBM per device.

v0:
```python
import functools
import math

import jax
import jax.numpy as jnp
from jax import lax
from jax.experimental import pallas as pl
from jax.experimental.pallas import tpu as pltpu
from jax.sharding import PartitionSpec as P

ITERS = 2
STATS = 8
MESH = pl.DeviceIdType.MESH
F32 = jnp.float32
BF16 = jnp.bfloat16

root_five = math.sqrt(5.0)
noise_level = 0.5


def halves(x):
    hi = x.astype(BF16)
    return hi, (x - hi.astype(F32)).astype(BF16)


def thirds(x):
    hi = x.astype(BF16)
    rest = x - hi.astype(F32)
    mid = rest.astype(BF16)
    return hi, mid, (rest - mid.astype(F32)).astype(BF16)


def dot_nn(a, b):
    return lax.dot_general(a, b, (((1,), (0,)), ((), ())), preferred_element_type=F32)


def dot_nt(a, b):
    return lax.dot_general(a, b, (((1,), (1,)), ((), ())), preferred_element_type=F32)


def fold(out):
    rows, width = out.shape[0] // 2, out.shape[1] // 2
    return (
        (out[rows:, width:] + out[:rows, width:]) + out[rows:, :width]
    ) + out[:rows, :width]


def stacked(x):
    return jnp.concatenate(halves(x), axis=0)


def kernel(
    n_row,
    n_col,
    low,
    rank,
    points_hbm,
    length_hbm,
    target_hbm,
    bits_hbm,
    leaf_hbm,
    top_hbm,
    sub_hbm,
    sol_ref,
    res_ref,
    coef_ref,
    points_ref,
    length_ref,
    bits_ref,
    leaf_ref,
    basis_ref,
    target_ref,
    rhs_ref,
    pts_line_ref,
    pts_plane_ref,
    line_ref,
    plane_ref,
    out_ref,
    kmat_ref,
    load_sem,
    send_sem,
    recv_sem,
):
    n_line = n_col // low
    n_plane = n_row * low
    row, col = lax.axis_index("row"), lax.axis_index("col")
    in_line = col // low
    lowest = lax.rem(col, low)
    in_plane = row * low + lowest
    cols, own = rhs_ref.shape
    dim = points_ref.shape[0]

    def line_peer(t):
        return row, lax.rem(in_line + t, n_line) * low + lowest

    def plane_slot(t):
        return lax.rem(in_plane + t, n_plane)

    def plane_peer(t):
        other = plane_slot(t)
        return other // low, in_line * low + lax.rem(other, low)

    loads = [
        pltpu.make_async_copy(src, dst, load_sem.at[at])
        for at, (src, dst) in enumerate(
            (
                (points_hbm, points_ref),
                (length_hbm, length_ref),
                (target_hbm, target_ref),
                (bits_hbm, bits_ref),
                (top_hbm, basis_ref.at[pl.ds(0, rank)]),
                (sub_hbm, basis_ref.at[pl.ds(rank, rank)]),
                (leaf_hbm, leaf_ref),
            )
        )
    ]
    for load in loads:
        load.start()

    barrier = pltpu.get_barrier_semaphore()
    for t in range(1, n_line):
        pl.semaphore_signal(barrier, inc=1, device_id=line_peer(t), device_id_type=MESH)
    for t in range(1, n_plane):
        pl.semaphore_signal(barrier, inc=1, device_id=plane_peer(t), device_id_type=MESH)

    def remote(src, dst, at, device):
        return pltpu.make_async_remote_copy(
            src_ref=src,
            dst_ref=dst,
            send_sem=send_sem.at[at],
            recv_sem=recv_sem.at[at],
            device_id=device,
            device_id_type=MESH,
        )

    def send_line(buf, at):
        for t in range(1, n_line):
            remote(buf.at[in_line], buf.at[in_line], at, line_peer(t)).start()

    def send_plane(buf, at):
        for t in range(1, n_plane):
            remote(buf.at[in_plane], buf.at[in_plane], at, plane_peer(t)).start()

    def all_line(buf, at):
        some = buf.at[pl.ds(0, n_line - 1)]
        return remote(some, some, at, line_peer(1))

    def all_plane(buf, at):
        some = buf.at[pl.ds(0, n_plane - 1)]
        return remote(some, some, at, plane_peer(1))

    eye = lax.broadcasted_iota(jnp.int32, (cols, own), 0) == lax.broadcasted_iota(
        jnp.int32, (cols, own), 1
    )
    stat_row = lax.broadcasted_iota(jnp.int32, (STATS, own), 0)
    is_top = lax.broadcasted_iota(jnp.int32, (cols, 2 * rank), 1) < rank

    def to_row(column):
        return jnp.sum(jnp.where(eye, column, 0.0), axis=0, keepdims=True)

    def to_col(line):
        return jnp.sum(jnp.where(eye, line, 0.0), axis=1, keepdims=True)

    def stats(*columns):
        out = jnp.zeros((STATS, own), F32)
        for at, column in enumerate(columns):
            out = jnp.where(stat_row == at, to_row(column), out)
        return out

    def dots(a, b):
        return jnp.sum(a * b, axis=1, keepdims=True)

    for load in loads[:4]:
        load.wait()
    rhs_ref[0:1, :] = target_ref[...]
    rhs_ref[1:cols, :] = 2.0 * bits_ref[...].astype(F32) - 1.0
    rhs = rhs_ref[...]
    inverse = jnp.sum(
        jnp.where(
            lax.broadcasted_iota(jnp.int32, (dim, dim), 0)
            == lax.broadcasted_iota(jnp.int32, (dim, dim), 1),
            length_ref[...],
            0.0,
        ),
        axis=1,
        keepdims=True,
    )
    scaled = points_ref[...] * inverse
    pts_line_ref[in_line] = scaled
    pts_plane_ref[in_plane] = scaled
    for load in loads[4:]:
        load.wait()
    basis_hi, basis_lo = halves(basis_ref[...])
    basis_tall = jnp.concatenate([basis_hi, basis_lo], axis=0)
    basis_wide = jnp.concatenate([basis_hi, basis_lo], axis=1)
    leaf_tall = stacked(leaf_ref[...])

    def project(v):
        return fold(dot_nt(stacked(v), basis_tall))

    def expand(c):
        return fold(dot_nn(stacked(c), basis_wide))

    def leaf(v):
        return fold(dot_nt(stacked(v), leaf_tall))

    def total(buf, first, count):
        out = buf[first]
        for i in range(first + 1, first + count):
            out = out + buf[i]
        return out

    def by_subtree(at):
        send_line(line_ref.at[at], 2 * at)
        yield
        all_line(line_ref.at[at], 2 * at).wait_recv()
        plane_ref[at, in_plane] = total(line_ref.at[at], 0, n_line)
        send_plane(plane_ref.at[at], 2 * at + 1)
        yield
        all_plane(plane_ref.at[at], 2 * at + 1).wait_recv()
        yield [total(plane_ref.at[at], i * low, low) for i in range(n_row)]

    def own_coef(parts):
        mine = parts[0]
        for i in range(1, n_row):
            mine = jnp.where(row == i, parts[i], mine)
        return jnp.where(is_top, sum(parts[1:], parts[0]), mine)

    def level_product(parts):
        every = sum(parts[1:], parts[0])
        squares = jnp.where(is_top, every * every, 0.0)
        for part in parts:
            squares = squares + jnp.where(is_top, 0.0, part * part)
        return jnp.sum(squares, axis=1, keepdims=True)

    line_ref[0, in_line, 0:cols, :] = project(rhs)
    leaf_res = leaf(rhs)
    line_ref[0, in_line, cols:, :] = stats(dots(rhs, leaf_res))
    pl.semaphore_wait(barrier, n_line + n_plane - 2)
    reduce = by_subtree(0)
    next(reduce)
    send_line(pts_line_ref, 10)
    send_plane(pts_plane_ref, 11)
    next(reduce)

    def norm_rows(sq, first):
        pieces = [p.astype(F32) for p in thirds(sq)]
        line = lax.broadcasted_iota(jnp.int32, (16, sq.shape[1]), 0)
        out = jnp.where((line >= 3 - 3 * first) & (line < 6 - 3 * first), 1.0, 0.0)
        for at, piece in enumerate(pieces):
            out = jnp.where(line == 3 * first + at, piece, out)
        return out.astype(BF16)

    def features(x, order, first):
        pieces = thirds(x)
        sq = jnp.sum(x * x, axis=0, keepdims=True)
        return [pieces[at] for at in order], norm_rows(sq, first)

    all_line(pts_line_ref, 10).wait_recv()
    sources = jnp.concatenate([pts_line_ref[i] for i in range(n_line)], axis=1)
    src_parts, src_norm = features(sources, (0, 0, 0, 1, 1, 2), 0)
    src_feat = jnp.concatenate(
        [-2.0 * p.astype(F32) for p in src_parts] + [src_norm.astype(F32)], axis=0
    ).T.astype(BF16)
    all_plane(pts_plane_ref, 11).wait_recv()

    sums = next(reduce)
    stat = sum([s[cols:] for s in sums[1:]], sums[0][cols:])
    parts = [s[0:cols] for s in sums]
    rz_now = to_col(stat[0:1]) + level_product(parts)
    direction = leaf_res + expand(own_coef(parts))
    line_ref[1, in_line, 0:cols, :] = direction
    line_ref[1, in_line, cols:, :] = jnp.zeros((STATS, own), F32)
    send_line(line_ref.at[1], 2)

    def build(q, carry):
        pair = jnp.concatenate(
            [pts_plane_ref[plane_slot(2 * q + 1)], pts_plane_ref[plane_slot(2 * q + 2)]], axis=1
        )
        far_parts, far_norm = features(pair, (0, 1, 2, 0, 1, 0), 1)
        far_feat = jnp.concatenate(far_parts + [far_norm], axis=0)
        for i in range(n_line):
            some = src_feat[i * own : (i + 1) * own]
            five_sq = jnp.maximum(5.0 * dot_nn(some, far_feat), 1e-30)
            dist = five_sq * lax.rsqrt(five_sq)
            value = (1.0 + dist + five_sq * (1.0 / 3.0)) * jnp.exp(-dist)
            hi, lo = halves(value)
            kmat_ref[q, i * own : (i + 1) * own, 0 : 2 * own] = hi
            kmat_ref[q, i * own : (i + 1) * own, 2 * own :] = lo
        return carry

    lax.fori_loop(0, n_plane // 2, build, 0)

    def apply_kernel(at):
        all_line(line_ref.at[at], 2 * at).wait_recv()
        mine = stacked(
            jnp.concatenate([line_ref[at, i, 0:cols, :] for i in range(n_line)], axis=1)
        )
        stat = total(line_ref.at[at, :, pl.ds(cols, STATS)], 0, n_line)
        for q in range(n_plane // 2):
            both = fold(dot_nn(mine, kmat_ref[q]))
            for half in range(2):
                t = 2 * q + 1 + half
                block = both[:, half * own : (half + 1) * own]
                if t == n_plane:
                    plane_ref[at, in_plane, 0:cols, :] = block
                    plane_ref[at, in_plane, cols:, :] = stat
                    continue
                slot = at // 2 * (n_plane - 1) + t - 1
                out_ref[slot, 0:cols, :] = block
                out_ref[slot, cols:, :] = stat
                remote(
                    out_ref.at[slot], plane_ref.at[at, in_plane], 2 * at + 1, plane_peer(t)
                ).start()
        all_plane(plane_ref.at[at], 2 * at + 1).wait_recv()
        both = total(plane_ref.at[at], 0, n_plane)
        return both[0:cols], both[cols:]

    image, _ = apply_kernel(1)
    image = image + noise_level * direction
    line_ref[2, in_line, 0:cols, :] = project(image)
    line_ref[2, in_line, cols:, :] = stats(dots(direction, image))
    reduce = by_subtree(2)
    next(reduce)
    leaf_image = leaf(image)
    next(reduce)
    sums = next(reduce)
    stat = sum([s[cols:] for s in sums[1:]], sums[0][cols:])
    alpha_0 = rz_now / to_col(stat[0:1])
    residual = rhs - alpha_0 * image
    leaf_res = leaf_res - alpha_0 * leaf_image
    parts = [a - alpha_0 * s[0:cols] for a, s in zip(parts, sums)]
    precond = leaf_res + expand(own_coef(parts))
    line_ref[3, in_line, 0:cols, :] = precond
    line_ref[3, in_line, cols:, :] = stats(dots(residual, leaf_res))
    send_line(line_ref.at[3], 6)
    answer = alpha_0 * direction
    levels = level_product(parts)

    product, stat = apply_kernel(3)
    leaf_total = to_col(stat[0:1])
    rz_next = leaf_total + levels
    beta_0 = rz_next / rz_now
    rz_now = rz_next
    direction = precond + beta_0 * direction
    image = product + noise_level * precond + beta_0 * image
    leaf_image = leaf(image)
    line_ref[4, in_line, 0:cols, :] = project(image)
    line_ref[4, in_line, cols:, :] = stats(
        dots(direction, image), dots(image, leaf_res), dots(image, leaf_image)
    )
    reduce = by_subtree(4)
    next(reduce)
    next(reduce)
    sums = next(reduce)
    stat = sum([s[cols:] for s in sums[1:]], sums[0][cols:])
    alpha_1 = rz_now / to_col(stat[0:1])
    sol_ref[...] = answer + alpha_1 * direction
    res_ref[...] = residual - alpha_1 * image
    parts = [a - alpha_1 * s[0:cols] for a, s in zip(parts, sums)]
    leaf_last = leaf_total - alpha_1 * (2.0 * to_col(stat[1:2]) - alpha_1 * to_col(stat[2:3]))
    beta_1 = (leaf_last + level_product(parts)) / rz_now
    for i, (alpha, beta) in enumerate(((alpha_0, beta_0), (alpha_1, beta_1))):
        coef_ref[0, i : i + 1, :] = to_row(alpha)[:, 0:cols]
        coef_ref[1, i : i + 1, :] = to_row(beta)[:, 0:cols]
    for at in range(5):
        all_line(line_ref.at[at], 2 * at).wait_send()
        all_plane(plane_ref.at[at], 2 * at + 1).wait_send()
    all_line(pts_line_ref, 10).wait_send()
    all_plane(pts_plane_ref, 11).wait_send()


def on_device(n_row, n_col, points, inverse_length, target, probe_bits, leaf_inverse, top_basis, sub_basis):
    low = math.gcd(n_col, 4)
    n_line, n_plane = n_col // low, n_row * low
    dim, own = points.shape
    cols = probe_bits.shape[0] + 1
    rank = top_basis.shape[0]
    vmem = pl.BlockSpec(memory_space=pltpu.VMEM)
    hbm = pl.BlockSpec(memory_space=pltpu.HBM)
    message = (cols + STATS, own)
    return pl.pallas_call(
        functools.partial(kernel, n_row, n_col, low, rank),
        out_shape=(
            jax.ShapeDtypeStruct((cols, own), F32),
            jax.ShapeDtypeStruct((cols, own), F32),
            jax.ShapeDtypeStruct((2, ITERS, cols), F32),
        ),
        in_specs=[hbm] * 7,
        out_specs=(vmem, vmem, vmem),
        scratch_shapes=[
            pltpu.VMEM(points.shape, F32),
            pltpu.VMEM((1, dim), F32),
            pltpu.VMEM(probe_bits.shape, jnp.int32),
            pltpu.VMEM(leaf_inverse.shape, F32),
            pltpu.VMEM((2 * rank, own), F32),
            pltpu.VMEM((1, own), F32),
            pltpu.VMEM((cols, own), F32),
            pltpu.VMEM((n_line, dim, own), F32),
            pltpu.VMEM((n_plane, dim, own), F32),
            pltpu.VMEM((5, n_line) + message, F32),
            pltpu.VMEM((5, n_plane) + message, F32),
            pltpu.VMEM((2 * (n_plane - 1),) + message, F32),
            pltpu.VMEM((n_plane // 2, n_line * own, 4 * own), BF16),
            pltpu.SemaphoreType.DMA((7,)),
            pltpu.SemaphoreType.DMA((12,)),
            pltpu.SemaphoreType.DMA((12,)),
        ],
        compiler_params=pltpu.CompilerParams(
            collective_id=0, has_side_effects=True, vmem_limit_bytes=48 * 1024 * 1024
        ),
    )(
        points,
        inverse_length.reshape(1, dim),
        target.reshape(1, own),
        probe_bits,
        leaf_inverse,
        top_basis,
        sub_basis,
    )


def solution(mesh):
    return jax.shard_map(
        functools.partial(on_device, mesh.shape["row"], mesh.shape["col"]),
        mesh=mesh,
        in_specs=(
            P(None, ("row", "col")),
            P(),
            P(("row", "col")),
            P(None, ("row", "col")),
            P(("row", "col"), None),
            P(None, ("row", "col")),
            P(None, ("row", "col")),
        ),
        out_specs=(P(None, ("row", "col")), P(None, ("row", "col")), P()),
        check_vma=False,
    )
```

profile of v0, /device:TPU:0, one launch (start us, length us, event | category | flops | bytes accessed | tf_op | source)
XLA Modules:
  0.0 49.2 jit_solution(13177079300449480281)
XLA Ops:
  0.6 0.0 copy-start.5
  0.6 0.0 copy-start.6
  0.7 0.6 %copy-done.5 = f32[16]{0:T(128)S(1)} copy-done((f32[16]{0:T(128)S(1)}, f32[16]{0:T(128)}, u32[]{:S(2)}) %copy-start.5) | copy-done | bytes 88
  1.3 0.0 copy-done.6
  1.3 0.0 copy-start
  1.3 0.8 %copy-done = f32[128,128]{1,0:T(8,128)S(1)} copy-done((f32[128,128]{1,0:T(8,128)S(1)}, f32[128,128]{1,0:T(8,128)}, u32[]{:S(2)}) %copy-start) | copy-done | bytes 65560
  2.1 0.0 copy-start.1
  2.1 0.8 %copy-done.1 = f32[64,128]{1,0:T(8,128)S(1)} copy-done((f32[64,128]{1,0:T(8,128)S(1)}, f32[64,128]{1,0:T(8,128)}, u32[]{:S(2)}) %copy-start.1) | copy-done | bytes 32792
  2.9 0.0 copy-start.2
  2.9 0.8 %copy-done.2 = f32[64,128]{1,0:T(8,128)S(1)} copy-done((f32[64,128]{1,0:T(8,128)S(1)}, f32[64,128]{1,0:T(8,128)}, u32[]{:S(2)}) %copy-start.2) | copy-done | bytes 32792
  3.7 0.0 copy-start.3
  3.7 0.7 %copy-done.3 = f32[16,128]{1,0:T(8,128)S(1)} copy-done((f32[16,128]{1,0:T(8,128)S(1)}, f32[16,128]{1,0:T(8,128)}, u32[]{:S(2)}) %copy-start.3) | copy-done | bytes 8216
  4.4 0.0 copy-start.4
  4.4 0.7 %copy-done.4 = s32[15,128]{1,0:T(8,128)S(1)} copy-done((s32[15,128]{1,0:T(8,128)S(1)}, s32[15,128]{1,0:T(8,128)}, u32[]{:S(2)}) %copy-start.4) | copy-done | bytes 7704
  5.1 42.4 %shard_map.94 = (f32[16,128]{1,0:T(8,128)S(1)}, f32[16,128]{1,0:T(8,128)S(1)}, f32[2,2,16]{2,1,0:T(2,128)S(1)}) custom-call(f32[16,128]{1,0:T(8,128)S(1)} %copy-done.3, f32[1,16]{1,0:T(1,128)S(1)} %bitcast.2, f32[1,128]{1,0:T(1,128)S(1)} %bitcast.3, s32[15,128]{1,0:T(8,128)S(1)} %copy-done.4, f32[128,128]{1,0:T(8,128)S(1)} %copy-done, ...), custom_call_target="tpu_custom_call" | custom-call | tf_op jit(solution)/shard_map/pallas_call | solution.py:382
  47.4 0.6 %copy.13 = f32[16,128]{1,0:T(8,128)} copy(f32[16,128]{1,0:T(8,128)S(1)} %get-tuple-element.6) | data formatting | bytes 16384
  48.0 0.6 %copy.14 = f32[16,128]{1,0:T(8,128)} copy(f32[16,128]{1,0:T(8,128)S(1)} %get-tuple-element.7) | data formatting | bytes 16384
  48.6 0.6 %copy.15 = f32[2,2,16]{2,1,0:T(2,128)} copy(f32[2,2,16]{2,1,0:T(2,128)S(1)} %get-tuple-element.8) | data formatting | bytes 512
Async XLA Ops:
  0.6 0.7 %copy-start.5 = (f32[16]{0:T(128)S(1)}, f32[16]{0:T(128)}, u32[]{:S(2)}) copy-start(f32[16]{0:T(128)} %param.8) | copy-start | bytes 196
  0.6 0.7 %copy-start.6 = (f32[128]{0:T(128)S(1)}, f32[128]{0:T(128)}, u32[]{:S(2)}) copy-start(f32[128]{0:T(128)} %param.9) | copy-start | bytes 1540
  1.3 0.8 %copy-start = (f32[128,128]{1,0:T(8,128)S(1)}, f32[128,128]{1,0:T(8,128)}, u32[]{:S(2)}) copy-start(f32[128,128]{1,0:T(8,128)} %leaf_hbm.1) | copy-start | bytes 196612
  2.1 0.8 %copy-start.1 = (f32[64,128]{1,0:T(8,128)S(1)}, f32[64,128]{1,0:T(8,128)}, u32[]{:S(2)}) copy-start(f32[64,128]{1,0:T(8,128)} %top_hbm.1) | copy-start | bytes 98308
  2.9 0.8 %copy-start.2 = (f32[64,128]{1,0:T(8,128)S(1)}, f32[64,128]{1,0:T(8,128)}, u32[]{:S(2)}) copy-start(f32[64,128]{1,0:T(8,128)} %sub_hbm.1) | copy-start | bytes 98308
  3.7 0.7 %copy-start.3 = (f32[16,128]{1,0:T(8,128)S(1)}, f32[16,128]{1,0:T(8,128)}, u32[]{:S(2)}) copy-start(f32[16,128]{1,0:T(8,128)} %points_hbm.1) | copy-start | bytes 24580
  4.4 0.7 %copy-start.4 = (s32[15,128]{1,0:T(8,128)S(1)}, s32[15,128]{1,0:T(8,128)}, u32[]{:S(2)}) copy-start(s32[15,128]{1,0:T(8,128)} %bits_hbm.1) | copy-start | bytes 23044
where the time goes:
time: 49.6 us; the launch traced here: 49.2 us
  Pallas kernels  42.4 us (85%)
  local copies, waits for them, and re-layouts  6.18 us (12%)
  between operations  0.66 us (1%)
    pallas_call x1, Pallas kernels, on_device(): pl.pallas_call(functools.partial(kernel, n_row, n_col, low, rank), out_sh...  42.4 us
    unnamed x17, local copies, waits for them, and re-layouts  6.18 us

commit v1 on v0

--- a/solution.py
+++ b/solution.py
@@ -69,36 +69,38 @@
     bits_ref,
     leaf_ref,
     basis_ref,
+    wide_ref,
     target_ref,
     rhs_ref,
     pts_line_ref,
     pts_plane_ref,
     line_ref,
     plane_ref,
+    prod_ref,
     out_ref,
     kmat_ref,
     load_sem,
     send_sem,
     recv_sem,
 ):
-    n_line = n_col // low
-    n_plane = n_row * low
+    n_high = n_col // low
+    n_line, n_plane = low, n_row * n_high
     row, col = lax.axis_index("row"), lax.axis_index("col")
-    in_line = col // low
-    lowest = lax.rem(col, low)
-    in_plane = row * low + lowest
+    high = col // low
+    in_line = lax.rem(col, low)
+    in_plane = row * n_high + high
     cols, own = rhs_ref.shape
     dim = points_ref.shape[0]
 
     def line_peer(t):
-        return row, lax.rem(in_line + t, n_line) * low + lowest
+        return row, high * low + lax.rem(in_line + t, n_line)
 
     def plane_slot(t):
         return lax.rem(in_plane + t, n_plane)
 
     def plane_peer(t):
         other = plane_slot(t)
-        return other // low, in_line * low + lax.rem(other, low)
+        return other // n_high, lax.rem(other, n_high) * low + in_line
 
     loads = [
         pltpu.make_async_copy(src, dst, load_sem.at[at])
@@ -108,8 +110,8 @@
                 (length_hbm, length_ref),
                 (target_hbm, target_ref),
                 (bits_hbm, bits_ref),
-                (top_hbm, basis_ref.at[pl.ds(0, rank)]),
-                (sub_hbm, basis_ref.at[pl.ds(rank, rank)]),
+                (top_hbm, basis_ref.at[in_line, pl.ds(0, rank)]),
+                (sub_hbm, basis_ref.at[in_line, pl.ds(rank, rank)]),
                 (leaf_hbm, leaf_ref),
             )
         )
@@ -134,12 +136,14 @@
         )
 
     def send_line(buf, at):
+        mine = buf.at[in_line]
         for t in range(1, n_line):
-            remote(buf.at[in_line], buf.at[in_line], at, line_peer(t)).start()
+            remote(mine, mine, at, line_peer(t)).start()
 
     def send_plane(buf, at):
+        mine = buf.at[in_plane]
         for t in range(1, n_plane):
-            remote(buf.at[in_plane], buf.at[in_plane], at, plane_peer(t)).start()
+            remote(mine, mine, at, plane_peer(t)).start()
 
     def all_line(buf, at):
         some = buf.at[pl.ds(0, n_line - 1)]
@@ -190,16 +194,14 @@
     pts_plane_ref[in_plane] = scaled
     for load in loads[4:]:
         load.wait()
-    basis_hi, basis_lo = halves(basis_ref[...])
-    basis_tall = jnp.concatenate([basis_hi, basis_lo], axis=0)
-    basis_wide = jnp.concatenate([basis_hi, basis_lo], axis=1)
+    basis_tall = stacked(basis_ref[in_line])
     leaf_tall = stacked(leaf_ref[...])
 
     def project(v):
         return fold(dot_nt(stacked(v), basis_tall))
 
     def expand(c):
-        return fold(dot_nn(stacked(c), basis_wide))
+        return fold(dot_nn(stacked(c), wide_ref[...]))
 
     def leaf(v):
         return fold(dot_nt(stacked(v), leaf_tall))
@@ -210,15 +212,36 @@
             out = out + buf[i]
         return out
 
-    def by_subtree(at):
-        send_line(line_ref.at[at], 2 * at)
+    def by_subtree(at, length):
+        message = line_ref.at[at, :, pl.ds(0, length)]
+        send_line(message, 2 * at)
         yield
-        all_line(line_ref.at[at], 2 * at).wait_recv()
-        plane_ref[at, in_plane] = total(line_ref.at[at], 0, n_line)
+        all_line(message, 2 * at).wait_recv()
+        plane_ref[at, in_plane] = total(line_ref.at[at, :, pl.ds(0, cols + STATS)], 0, n_line)
         send_plane(plane_ref.at[at], 2 * at + 1)
         yield
         all_plane(plane_ref.at[at], 2 * at + 1).wait_recv()
-        yield [total(plane_ref.at[at], i * low, low) for i in range(n_row)]
+        sums = [total(plane_ref.at[at], i * n_high, n_high) for i in range(n_row)]
+        yield [s[0:cols] for s in sums], sum([s[cols:] for s in sums[1:]], sums[0][cols:])
+
+    def put(at, vector, columns, *more):
+        line_ref[at, in_line, 0:cols, :] = project(vector)
+        line_ref[at, in_line, cols : cols + STATS, :] = stats(*columns)
+        for i, part in enumerate(more):
+            first = cols + STATS + i * cols
+            line_ref[at, in_line, first : first + cols, :] = part
+
+    def of_line(at, which):
+        first = cols + STATS + which * cols
+        return jnp.concatenate(
+            [line_ref[at, i, first : first + cols, :] for i in range(n_line)], axis=1
+        )
+
+    def pick(lanes):
+        mine = lanes[:, 0:own]
+        for i in range(1, n_line):
+            mine = jnp.where(in_line == i, lanes[:, i * own : (i + 1) * own], mine)
+        return mine
 
     def own_coef(parts):
         mine = parts[0]
@@ -233,14 +256,15 @@
             squares = squares + jnp.where(is_top, 0.0, part * part)
         return jnp.sum(squares, axis=1, keepdims=True)
 
-    line_ref[0, in_line, 0:cols, :] = project(rhs)
+    long = cols + STATS + 2 * cols
     leaf_res = leaf(rhs)
-    line_ref[0, in_line, cols:, :] = stats(dots(rhs, leaf_res))
+    put(0, rhs, (dots(rhs, leaf_res),), leaf_res, rhs)
     pl.semaphore_wait(barrier, n_line + n_plane - 2)
-    reduce = by_subtree(0)
-    next(reduce)
-    send_line(pts_line_ref, 10)
-    send_plane(pts_plane_ref, 11)
+    reduce = by_subtree(0, long)
+    next(reduce)
+    send_line(pts_line_ref, 6)
+    send_plane(pts_plane_ref, 7)
+    send_line(basis_ref, 8)
     next(reduce)
 
     def norm_rows(sq, first):
@@ -256,22 +280,13 @@
         sq = jnp.sum(x * x, axis=0, keepdims=True)
         return [pieces[at] for at in order], norm_rows(sq, first)
 
-    all_line(pts_line_ref, 10).wait_recv()
+    all_line(pts_line_ref, 6).wait_recv()
     sources = jnp.concatenate([pts_line_ref[i] for i in range(n_line)], axis=1)
     src_parts, src_norm = features(sources, (0, 0, 0, 1, 1, 2), 0)
     src_feat = jnp.concatenate(
         [-2.0 * p.astype(F32) for p in src_parts] + [src_norm.astype(F32)], axis=0
     ).T.astype(BF16)
-    all_plane(pts_plane_ref, 11).wait_recv()
-
-    sums = next(reduce)
-    stat = sum([s[cols:] for s in sums[1:]], sums[0][cols:])
-    parts = [s[0:cols] for s in sums]
-    rz_now = to_col(stat[0:1]) + level_product(parts)
-    direction = leaf_res + expand(own_coef(parts))
-    line_ref[1, in_line, 0:cols, :] = direction
-    line_ref[1, in_line, cols:, :] = jnp.zeros((STATS, own), F32)
-    send_line(line_ref.at[1], 2)
+    all_plane(pts_plane_ref, 7).wait_recv()
 
     def build(q, carry):
         pair = jnp.concatenate(
@@ -291,88 +306,100 @@
 
     lax.fori_loop(0, n_plane // 2, build, 0)
 
-    def apply_kernel(at):
-        all_line(line_ref.at[at], 2 * at).wait_recv()
-        mine = stacked(
-            jnp.concatenate([line_ref[at, i, 0:cols, :] for i in range(n_line)], axis=1)
-        )
-        stat = total(line_ref.at[at, :, pl.ds(cols, STATS)], 0, n_line)
+    all_line(basis_ref, 8).wait_recv()
+    for i in range(n_line):
+        hi, lo = halves(basis_ref[i])
+        wide_ref[:, i * own : (i + 1) * own] = hi
+        wide_ref[:, (n_line + i) * own : (n_line + i + 1) * own] = lo
+
+    def apply_kernel(which, vectors, stat):
+        at = 9 + which
+        mine = stacked(vectors)
+        length = cols if stat is None else cols + STATS
+        inbox = prod_ref.at[which, :, pl.ds(0, length)]
         for q in range(n_plane // 2):
             both = fold(dot_nn(mine, kmat_ref[q]))
             for half in range(2):
                 t = 2 * q + 1 + half
                 block = both[:, half * own : (half + 1) * own]
                 if t == n_plane:
-                    plane_ref[at, in_plane, 0:cols, :] = block
-                    plane_ref[at, in_plane, cols:, :] = stat
+                    prod_ref[which, in_plane, 0:cols, :] = block
+                    if stat is not None:
+                        prod_ref[which, in_plane, cols:, :] = stat
                     continue
-                slot = at // 2 * (n_plane - 1) + t - 1
+                slot = which * (n_plane - 1) + t - 1
                 out_ref[slot, 0:cols, :] = block
-                out_ref[slot, cols:, :] = stat
+                if stat is not None:
+                    out_ref[slot, cols:, :] = stat
                 remote(
-                    out_ref.at[slot], plane_ref.at[at, in_plane], 2 * at + 1, plane_peer(t)
+                    out_ref.at[slot, pl.ds(0, length)],
+                    inbox.at[in_plane],
+                    at,
+                    plane_peer(t),
                 ).start()
-        all_plane(plane_ref.at[at], 2 * at + 1).wait_recv()
-        both = total(plane_ref.at[at], 0, n_plane)
-        return both[0:cols], both[cols:]
-
-    image, _ = apply_kernel(1)
-    image = image + noise_level * direction
-    line_ref[2, in_line, 0:cols, :] = project(image)
-    line_ref[2, in_line, cols:, :] = stats(dots(direction, image))
-    reduce = by_subtree(2)
-    next(reduce)
+        all_plane(inbox, at).wait_recv()
+        return total(inbox, 0, n_plane)
+
+    parts, stat = next(reduce)
+    rz_now = to_col(stat[0:1]) + level_product(parts)
+    leaf_lanes = of_line(0, 0)
+    lanes = leaf_lanes + expand(own_coef(parts))
+    direction = pick(lanes)
+
+    image = apply_kernel(0, lanes, None) + noise_level * direction
     leaf_image = leaf(image)
-    next(reduce)
-    sums = next(reduce)
-    stat = sum([s[cols:] for s in sums[1:]], sums[0][cols:])
+    put(1, image, (dots(direction, image),), leaf_image, image)
+    reduce = by_subtree(1, long)
+    next(reduce)
+    next(reduce)
+    sums, stat = next(reduce)
     alpha_0 = rz_now / to_col(stat[0:1])
+    parts = [a - alpha_0 * s for a, s in zip(parts, sums)]
+    leaf_lanes = leaf_lanes - alpha_0 * of_line(1, 0)
+    lanes = leaf_lanes + expand(own_coef(parts))
+    leaf_prod = dots(of_line(0, 1) - alpha_0 * of_line(1, 1), leaf_lanes)
+
+    product = apply_kernel(1, lanes, stats(leaf_prod))
+    answer = alpha_0 * direction
     residual = rhs - alpha_0 * image
     leaf_res = leaf_res - alpha_0 * leaf_image
-    parts = [a - alpha_0 * s[0:cols] for a, s in zip(parts, sums)]
-    precond = leaf_res + expand(own_coef(parts))
-    line_ref[3, in_line, 0:cols, :] = precond
-    line_ref[3, in_line, cols:, :] = stats(dots(residual, leaf_res))
-    send_line(line_ref.at[3], 6)
-    answer = alpha_0 * direction
-    levels = level_product(parts)
-
-    product, stat = apply_kernel(3)
-    leaf_total = to_col(stat[0:1])
-    rz_next = leaf_total + levels
+    precond = pick(lanes)
+    leaf_total = to_col(product[cols : cols + 1])
+    rz_next = leaf_total + level_product(parts)
     beta_0 = rz_next / rz_now
     rz_now = rz_next
     direction = precond + beta_0 * direction
-    image = product + noise_level * precond + beta_0 * image
+    image = product[0:cols] + noise_level * precond + beta_0 * image
     leaf_image = leaf(image)
-    line_ref[4, in_line, 0:cols, :] = project(image)
-    line_ref[4, in_line, cols:, :] = stats(
-        dots(direction, image), dots(image, leaf_res), dots(image, leaf_image)
-    )
-    reduce = by_subtree(4)
-    next(reduce)
-    next(reduce)
-    sums = next(reduce)
-    stat = sum([s[cols:] for s in sums[1:]], sums[0][cols:])
+    put(2, image, (dots(direction, image), dots(image, leaf_res), dots(image, leaf_image)))
+    reduce = by_subtree(2, cols + STATS)
+    next(reduce)
+    next(reduce)
+    sums, stat = next(reduce)
     alpha_1 = rz_now / to_col(stat[0:1])
     sol_ref[...] = answer + alpha_1 * direction
     res_ref[...] = residual - alpha_1 * image
-    parts = [a - alpha_1 * s[0:cols] for a, s in zip(parts, sums)]
+    parts = [a - alpha_1 * s for a, s in zip(parts, sums)]
     leaf_last = leaf_total - alpha_1 * (2.0 * to_col(stat[1:2]) - alpha_1 * to_col(stat[2:3]))
     beta_1 = (leaf_last + level_product(parts)) / rz_now
     for i, (alpha, beta) in enumerate(((alpha_0, beta_0), (alpha_1, beta_1))):
         coef_ref[0, i : i + 1, :] = to_row(alpha)[:, 0:cols]
         coef_ref[1, i : i + 1, :] = to_row(beta)[:, 0:cols]
-    for at in range(5):
-        all_line(line_ref.at[at], 2 * at).wait_send()
+    for at in range(3):
+        length = long if at < 2 else cols + STATS
+        all_line(line_ref.at[at, :, pl.ds(0, length)], 2 * at).wait_send()
         all_plane(plane_ref.at[at], 2 * at + 1).wait_send()
-    all_line(pts_line_ref, 10).wait_send()
-    all_plane(pts_plane_ref, 11).wait_send()
+    for which in range(2):
+        length = cols if which == 0 else cols + STATS
+        all_plane(prod_ref.at[which, :, pl.ds(0, length)], 9 + which).wait_send()
+    all_line(pts_line_ref, 6).wait_send()
+    all_plane(pts_plane_ref, 7).wait_send()
+    all_line(basis_ref, 8).wait_send()
 
 
 def on_device(n_row, n_col, points, inverse_length, target, probe_bits, leaf_inverse, top_basis, sub_basis):
     low = math.gcd(n_col, 4)
-    n_line, n_plane = n_col // low, n_row * low
+    n_line, n_plane = low, n_row * (n_col // low)
     dim, own = points.shape
     cols = probe_bits.shape[0] + 1
     rank = top_basis.shape[0]
@@ -393,21 +420,23 @@
             pltpu.VMEM((1, dim), F32),
             pltpu.VMEM(probe_bits.shape, jnp.int32),
             pltpu.VMEM(leaf_inverse.shape, F32),
-            pltpu.VMEM((2 * rank, own), F32),
+            pltpu.VMEM((n_line, 2 * rank, own), F32),
+            pltpu.VMEM((2 * rank, 2 * n_line * own), BF16),
             pltpu.VMEM((1, own), F32),
             pltpu.VMEM((cols, own), F32),
             pltpu.VMEM((n_line, dim, own), F32),
             pltpu.VMEM((n_plane, dim, own), F32),
-            pltpu.VMEM((5, n_line) + message, F32),
-            pltpu.VMEM((5, n_plane) + message, F32),
+            pltpu.VMEM((3, n_line, STATS + 3 * cols, own), F32),
+            pltpu.VMEM((3, n_plane) + message, F32),
+            pltpu.VMEM((2, n_plane) + message, F32),
             pltpu.VMEM((2 * (n_plane - 1),) + message, F32),
             pltpu.VMEM((n_plane // 2, n_line * own, 4 * own), BF16),
             pltpu.SemaphoreType.DMA((7,)),
-            pltpu.SemaphoreType.DMA((12,)),
-            pltpu.SemaphoreType.DMA((12,)),
+            pltpu.SemaphoreType.DMA((11,)),
+            pltpu.SemaphoreType.DMA((11,)),
         ],
         compiler_params=pltpu.CompilerParams(
-            collective_id=0, has_side_effects=True, vmem_limit_bytes=48 * 1024 * 1024
+            collective_id=0, has_side_effects=True, vmem_limit_bytes=62 * 1024 * 1024
         ),
     )(
         points,

time: 49.6 us -> 43.3 us (0.87)
  local copies, waits for them, and re-layouts: 6.18 us -> 2.55 us
  Pallas kernels: 42.4 us -> 39.8 us
    unnamed x17 -> x7, local copies, waits for them, and re-layouts: 6.18 us -> 2.55 us
    pallas_call x1, Pallas kernels: 42.4 us -> 39.8 us  [on_device(): pl.pallas_call(functools.partial(kernel, n_row, n_col, low, rank), out_sh...]
where the time goes in v1:
time: 43.3 us; the launch traced here: 43 us
  Pallas kernels  39.8 us (92%)
  local copies, waits for them, and re-layouts  2.55 us (6%)
  between operations  0.65 us (2%)
    pallas_call x1, Pallas kernels, on_device(): pl.pallas_call(functools.partial(kernel, n_row, n_col, low, rank), out_sh...  39.8 us
    unnamed x7, local copies, waits for them, and re-layouts  2.55 us

profile of v1, /device:TPU:0, one launch (start us, length us, event | category | flops | bytes accessed | tf_op | source)
XLA Modules:
  0.0 43.0 jit_solution(17980790103130434389)
XLA Ops:
  0.6 39.8 %shard_map.94 = (f32[16,128]{1,0:T(8,128)}, f32[16,128]{1,0:T(8,128)}, f32[2,2,16]{2,1,0:T(2,128)}) custom-call(f32[16,128]{1,0:T(8,128)} %points_hbm.1, f32[1,16]{1,0:T(1,128)} %bitcast.2, f32[1,128]{1,0:T(1,128)} %bitcast.3, s32[15,128]{1,0:T(8,128)} %bits_hbm.1, f32[128,128]{1,0:T(8,128)} %leaf_hbm.1, f32[64,128]{1,0:T(8,128)} %top_hbm.1, f32[64,128]{1,0:T(8,128)} %sub_hbm.1), custom_call_target="tpu_custom_call" | custom-call | tf_op jit(solution)/shard_map/pallas_call | solution.py:409
  40.4 0.0 copy-start
  40.4 1.3 %copy.13 = f32[16,128]{1,0:T(8,128)} copy(f32[16,128]{1,0:T(8,128)} %get-tuple-element.6) | data formatting | bytes 16384
  41.7 0.0 copy-done
  41.7 0.0 copy-start.1
  41.7 0.6 %copy.14 = f32[16,128]{1,0:T(8,128)} copy(f32[16,128]{1,0:T(8,128)S(1)} %copy-done) | data formatting | bytes 16384
  42.3 0.1 copy-done.1
  42.4 0.6 %copy.15 = f32[2,2,16]{2,1,0:T(2,128)} copy(f32[2,2,16]{2,1,0:T(2,128)S(1)} %copy-done.1) | data formatting | bytes 512
Async XLA Ops:
  40.4 1.3 %copy-start = (f32[16,128]{1,0:T(8,128)S(1)}, f32[16,128]{1,0:T(8,128)}, u32[]{:S(2)}) copy-start(f32[16,128]{1,0:T(8,128)} %get-tuple-element.7) | copy-start | bytes 24580
  41.7 0.7 %copy-start.1 = (f32[2,2,16]{2,1,0:T(2,128)S(1)}, f32[2,2,16]{2,1,0:T(2,128)}, u32[]{:S(2)}) copy-start(f32[2,2,16]{2,1,0:T(2,128)} %get-tuple-element.8) | copy-start | bytes 772

commit v2 on v1

v2 whole, which is shorter than its diff:
```python
import functools
import math

import jax
import jax.numpy as jnp
from jax import lax
from jax.experimental import pallas as pl
from jax.experimental.pallas import tpu as pltpu
from jax.sharding import PartitionSpec as P

ITERS = 2
MESH = pl.DeviceIdType.MESH
F32 = jnp.float32
BF16 = jnp.bfloat16

root_five = math.sqrt(5.0)
noise_level = 0.5


def halves(x):
    hi = x.astype(BF16)
    return hi, (x - hi.astype(F32)).astype(BF16)


def thirds(x):
    hi = x.astype(BF16)
    rest = x - hi.astype(F32)
    mid = rest.astype(BF16)
    return hi, mid, (rest - mid.astype(F32)).astype(BF16)


def dot_nn(a, b):
    return lax.dot_general(a, b, (((1,), (0,)), ((), ())), preferred_element_type=F32)


def dot_nt(a, b):
    return lax.dot_general(a, b, (((1,), (1,)), ((), ())), preferred_element_type=F32)


def fold(out):
    rows, width = out.shape[0] // 2, out.shape[1] // 2
    return (
        (out[rows:, width:] + out[:rows, width:]) + out[rows:, :width]
    ) + out[:rows, :width]


def stacked(x):
    return jnp.concatenate(halves(x), axis=0)


def kernel(
    n_row,
    n_col,
    low,
    rank,
    points_hbm,
    length_hbm,
    target_hbm,
    bits_hbm,
    leaf_hbm,
    top_hbm,
    sub_hbm,
    sol_ref,
    res_ref,
    coef_ref,
    points_ref,
    length_ref,
    bits_ref,
    leaf_ref,
    basis_ref,
    wide_ref,
    target_ref,
    rhs_ref,
    pts_line_ref,
    pts_plane_ref,
    line_ref,
    line_stat_ref,
    extra_ref,
    plane_ref,
    plane_stat_ref,
    prod_ref,
    prod_stat_ref,
    out_ref,
    kmat_ref,
    load_sem,
    send_sem,
    recv_sem,
):
    n_high = n_col // low
    n_line, n_plane = low, n_row * n_high
    row, col = lax.axis_index("row"), lax.axis_index("col")
    high = lax.div(col, low)
    in_line = lax.rem(col, low)
    in_plane = row * n_high + high
    cols, own = rhs_ref.shape
    dim = points_ref.shape[0]

    line_peers = [(row, high * low + lax.rem(in_line + t, n_line)) for t in range(1, n_line)]
    plane_slots = [lax.rem(in_plane + t, n_plane) for t in range(n_plane)]
    plane_peers = [
        (lax.div(slot, n_high), lax.rem(slot, n_high) * low + in_line) for slot in plane_slots[1:]
    ]

    loads = [
        pltpu.make_async_copy(src, dst, load_sem.at[at])
        for at, (src, dst) in enumerate(
            (
                (points_hbm, points_ref),
                (length_hbm, length_ref),
                (target_hbm, target_ref),
                (bits_hbm, bits_ref),
                (top_hbm, basis_ref.at[in_line, pl.ds(0, rank)]),
                (sub_hbm, basis_ref.at[in_line, pl.ds(rank, rank)]),
                (leaf_hbm, leaf_ref),
            )
        )
    ]
    for load in loads:
        load.start()

    barrier = pltpu.get_barrier_semaphore()
    for peer in line_peers + plane_peers:
        pl.semaphore_signal(barrier, inc=1, device_id=peer, device_id_type=MESH)

    def remote(src, dst, at, device):
        return pltpu.make_async_remote_copy(
            src_ref=src,
            dst_ref=dst,
            send_sem=send_sem.at[at],
            recv_sem=recv_sem.at[at],
            device_id=device,
            device_id_type=MESH,
        )

    def send_line(buf, at):
        mine = buf.at[in_line]
        for peer in line_peers:
            remote(mine, mine, at, peer).start()

    def send_plane(buf, at):
        mine = buf.at[in_plane]
        for peer in plane_peers:
            remote(mine, mine, at, peer).start()

    def all_line(buf, at):
        some = buf.at[pl.ds(0, n_line - 1)]
        return remote(some, some, at, line_peers[0])

    def all_plane(buf, at):
        some = buf.at[pl.ds(0, n_plane - 1)]
        return remote(some, some, at, plane_peers[0])

    offset = lax.broadcasted_iota(jnp.int32, (cols, own), 1) - lax.broadcasted_iota(
        jnp.int32, (cols, own), 0
    )
    is_top = lax.broadcasted_iota(jnp.int32, (cols, 2 * rank), 1) < rank

    def to_row(*columns):
        spread = jnp.zeros((cols, own), F32)
        for at, column in enumerate(columns):
            spread = jnp.where(offset == at * cols, column, spread)
        return jnp.sum(spread, axis=0, keepdims=True)

    def to_col(line, at=0):
        return jnp.sum(jnp.where(offset == at * cols, line, 0.0), axis=1, keepdims=True)

    def dots(a, b):
        return jnp.sum(a * b, axis=1, keepdims=True)

    for load in loads[:4]:
        load.wait()
    rhs_ref[0:1, :] = target_ref[...]
    rhs_ref[1:cols, :] = 2.0 * bits_ref[...].astype(F32) - 1.0
    rhs = rhs_ref[...]
    inverse = jnp.sum(
        jnp.where(
            lax.broadcasted_iota(jnp.int32, (dim, dim), 0)
            == lax.broadcasted_iota(jnp.int32, (dim, dim), 1),
            length_ref[...],
            0.0,
        ),
        axis=1,
        keepdims=True,
    )
    scaled = points_ref[...] * inverse
    pts_line_ref[in_line] = scaled
    pts_plane_ref[in_plane] = scaled
    for load in loads[4:]:
        load.wait()
    basis_tall = stacked(basis_ref[in_line])
    leaf_tall = stacked(leaf_ref[...])

    def project(v):
        return fold(dot_nt(stacked(v), basis_tall))

    def expand(c):
        return fold(dot_nn(stacked(c), wide_ref[...]))

    def leaf(v):
        return fold(dot_nt(stacked(v), leaf_tall))

    def total(buf, first, count):
        out = buf[first]
        for i in range(first + 1, first + count):
            out = out + buf[i]
        return out

    def send_coef(at, vector):
        line_ref[at, in_line] = project(vector)
        send_line(line_ref.at[at], 4 * at)

    def send_stat(at, *columns):
        line_stat_ref[at, in_line] = to_row(*columns)
        send_line(line_stat_ref.at[at], 4 * at + 1)

    def send_extra(at, *more):
        for i, part in enumerate(more):
            extra_ref[at, in_line, i * cols : (i + 1) * cols, :] = part
        send_line(extra_ref.at[at], 12 + at)

    def cross(at):
        all_line(line_ref.at[at], 4 * at).wait_recv()
        plane_ref[at, in_plane] = total(line_ref.at[at], 0, n_line)
        send_plane(plane_ref.at[at], 4 * at + 2)
        all_line(line_stat_ref.at[at], 4 * at + 1).wait_recv()
        plane_stat_ref[at, in_plane] = total(line_stat_ref.at[at], 0, n_line)
        send_plane(plane_stat_ref.at[at], 4 * at + 3)

    def by_subtree(at):
        all_plane(plane_ref.at[at], 4 * at + 2).wait_recv()
        return [total(plane_ref.at[at], i * n_high, n_high) for i in range(n_row)]

    def all_stats(at):
        all_plane(plane_stat_ref.at[at], 4 * at + 3).wait_recv()
        return total(plane_stat_ref.at[at], 0, n_plane)

    def of_line(at, which):
        rows = slice(which * cols, (which + 1) * cols)
        return jnp.concatenate([extra_ref[at, i, rows, :] for i in range(n_line)], axis=1)

    def pick(lanes):
        mine = lanes[:, 0:own]
        for i in range(1, n_line):
            mine = jnp.where(in_line == i, lanes[:, i * own : (i + 1) * own], mine)
        return mine

    def own_coef(parts):
        mine = parts[0]
        for i in range(1, n_row):
            mine = jnp.where(row == i, parts[i], mine)
        return jnp.where(is_top, sum(parts[1:], parts[0]), mine)

    def level_product(parts):
        every = sum(parts[1:], parts[0])
        squares = jnp.where(is_top, every * every, 0.0)
        for part in parts:
            squares = squares + jnp.where(is_top, 0.0, part * part)
        return jnp.sum(squares, axis=1, keepdims=True)

    line_ref[0, in_line] = project(rhs)
    leaf_res = leaf(rhs)
    line_stat_ref[0, in_line] = to_row(dots(rhs, leaf_res))
    pl.semaphore_wait(barrier, n_line + n_plane - 2)
    send_line(line_ref.at[0], 0)
    send_line(line_stat_ref.at[0], 1)
    send_line(pts_line_ref, 14)
    send_plane(pts_plane_ref, 15)
    send_extra(0, leaf_res, rhs)
    send_line(basis_ref, 16)

    def norm_rows(sq, first):
        pieces = [p.astype(F32) for p in thirds(sq)]
        line = lax.broadcasted_iota(jnp.int32, (16, sq.shape[1]), 0)
        out = jnp.where((line >= 3 - 3 * first) & (line < 6 - 3 * first), 1.0, 0.0)
        for at, piece in enumerate(pieces):
            out = jnp.where(line == 3 * first + at, piece, out)
        return out.astype(BF16)

    def features(x, order, first):
        pieces = thirds(x)
        sq = jnp.sum(x * x, axis=0, keepdims=True)
        return [pieces[at] for at in order], norm_rows(sq, first)

    all_line(pts_line_ref, 14).wait_recv()
    sources = jnp.concatenate([pts_line_ref[i] for i in range(n_line)], axis=1)
    src_parts, src_norm = features(sources, (0, 0, 0, 1, 1, 2), 0)
    src_feat = jnp.concatenate(
        [-2.0 * p.astype(F32) for p in src_parts] + [src_norm.astype(F32)], axis=0
    ).T.astype(BF16)
    cross(0)
    all_plane(pts_plane_ref, 15).wait_recv()

    def build(q, carry):
        pair = jnp.concatenate(
            [pts_plane_ref[lax.rem(in_plane + 2 * q + i, n_plane)] for i in (1, 2)], axis=1
        )
        far_parts, far_norm = features(pair, (0, 1, 2, 0, 1, 0), 1)
        far_feat = jnp.concatenate(far_parts + [far_norm], axis=0)
        for i in range(n_line):
            some = src_feat[i * own : (i + 1) * own]
            five_sq = jnp.maximum(5.0 * dot_nn(some, far_feat), 1e-30)
            dist = five_sq * lax.rsqrt(five_sq)
            value = (1.0 + dist + five_sq * (1.0 / 3.0)) * jnp.exp(-dist)
            hi, lo = halves(value)
            kmat_ref[q, i * own : (i + 1) * own, 0 : 2 * own] = hi
            kmat_ref[q, i * own : (i + 1) * own, 2 * own :] = lo
        return carry

    lax.fori_loop(0, n_plane // 2, build, 0)

    all_line(basis_ref, 16).wait_recv()
    for i in range(n_line):
        hi, lo = halves(basis_ref[i])
        wide_ref[:, i * own : (i + 1) * own] = hi
        wide_ref[:, (n_line + i) * own : (n_line + i + 1) * own] = lo

    def send_products(which, vectors):
        mine = stacked(vectors)
        for q in range(n_plane // 2):
            both = fold(dot_nn(mine, kmat_ref[q]))
            for half in range(2):
                t = 2 * q + 1 + half
                block = both[:, half * own : (half + 1) * own]
                if t == n_plane:
                    prod_ref[which, in_plane] = block
                    continue
                slot = which * (n_plane - 1) + t - 1
                out_ref[slot] = block
                remote(
                    out_ref.at[slot], prod_ref.at[which, in_plane], 17 + which, plane_peers[t - 1]
                ).start()

    def products(which):
        all_plane(prod_ref.at[which], 17 + which).wait_recv()
        return total(prod_ref.at[which], 0, n_plane)

    all_line(extra_ref.at[0], 12).wait_recv()
    leaf_lanes = of_line(0, 0)
    parts = by_subtree(0)
    lanes = leaf_lanes + expand(own_coef(parts))
    send_products(0, lanes)
    direction = pick(lanes)
    rz_now = to_col(all_stats(0)) + level_product(parts)

    image = products(0) + noise_level * direction
    send_coef(1, image)
    send_stat(1, dots(direction, image))
    leaf_image = leaf(image)
    send_extra(1, leaf_image, image)
    cross(1)
    all_line(extra_ref.at[1], 13).wait_recv()
    leaf_step = of_line(1, 0)
    alpha_0 = rz_now / to_col(all_stats(1))
    sums = by_subtree(1)
    parts = [a - alpha_0 * s for a, s in zip(parts, sums)]
    leaf_lanes = leaf_lanes - alpha_0 * leaf_step
    lanes = leaf_lanes + expand(own_coef(parts))
    send_products(1, lanes)
    residual_lanes = of_line(0, 1) - alpha_0 * of_line(1, 1)
    prod_stat_ref[in_plane] = to_row(dots(residual_lanes, leaf_lanes))
    send_plane(prod_stat_ref, 19)
    answer = alpha_0 * direction
    residual = rhs - alpha_0 * image
    leaf_res = leaf_res - alpha_0 * leaf_image
    precond = pick(lanes)
    levels = level_product(parts)

    all_plane(prod_stat_ref, 19).wait_recv()
    leaf_total = to_col(total(prod_stat_ref, 0, n_plane))
    rz_next = leaf_total + levels
    beta_0 = rz_next / rz_now
    rz_now = rz_next
    direction = precond + beta_0 * direction
    rest = noise_level * precond + beta_0 * image
    image = products(1) + rest
    send_coef(2, image)
    leaf_image = leaf(image)
    send_stat(2, dots(direction, image), dots(image, leaf_res), dots(image, leaf_image))
    cross(2)
    stat = all_stats(2)
    alpha_1 = rz_now / to_col(stat)
    sol_ref[...] = answer + alpha_1 * direction
    res_ref[...] = residual - alpha_1 * image
    leaf_last = leaf_total - alpha_1 * (2.0 * to_col(stat, 1) - alpha_1 * to_col(stat, 2))
    parts = [a - alpha_1 * s for a, s in zip(parts, by_subtree(2))]
    beta_1 = (leaf_last + level_product(parts)) / rz_now
    for i, (alpha, beta) in enumerate(((alpha_0, beta_0), (alpha_1, beta_1))):
        coef_ref[0, i : i + 1, :] = to_row(alpha)[:, 0:cols]
        coef_ref[1, i : i + 1, :] = to_row(beta)[:, 0:cols]
    for at in range(3):
        all_line(line_ref.at[at], 4 * at).wait_send()
        all_line(line_stat_ref.at[at], 4 * at + 1).wait_send()
        all_plane(plane_ref.at[at], 4 * at + 2).wait_send()
        all_plane(plane_stat_ref.at[at], 4 * at + 3).wait_send()
    for at in range(2):
        all_line(extra_ref.at[at], 12 + at).wait_send()
        all_plane(prod_ref.at[at], 17 + at).wait_send()
    all_line(pts_line_ref, 14).wait_send()
    all_plane(pts_plane_ref, 15).wait_send()
    all_line(basis_ref, 16).wait_send()
    all_plane(prod_stat_ref, 19).wait_send()


def on_device(n_row, n_col, points, inverse_length, target, probe_bits, leaf_inverse, top_basis, sub_basis):
    low = math.gcd(n_col, 4)
    n_line, n_plane = low, n_row * (n_col // low)
    dim, own = points.shape
    cols = probe_bits.shape[0] + 1
    rank = top_basis.shape[0]
    vmem = pl.BlockSpec(memory_space=pltpu.VMEM)
    hbm = pl.BlockSpec(memory_space=pltpu.HBM)
    message = (cols, own)
    return pl.pallas_call(
        functools.partial(kernel, n_row, n_col, low, rank),
        out_shape=(
            jax.ShapeDtypeStruct((cols, own), F32),
            jax.ShapeDtypeStruct((cols, own), F32),
            jax.ShapeDtypeStruct((2, ITERS, cols), F32),
        ),
        in_specs=[hbm] * 7,
        out_specs=(vmem, vmem, vmem),
        scratch_shapes=[
            pltpu.VMEM(points.shape, F32),
            pltpu.VMEM((1, dim), F32),
            pltpu.VMEM(probe_bits.shape, jnp.int32),
            pltpu.VMEM(leaf_inverse.shape, F32),
            pltpu.VMEM((n_line, 2 * rank, own), F32),
            pltpu.VMEM((2 * rank, 2 * n_line * own), BF16),
            pltpu.VMEM((1, own), F32),
            pltpu.VMEM((cols, own), F32),
            pltpu.VMEM((n_line, dim, own), F32),
            pltpu.VMEM((n_plane, dim, own), F32),
            pltpu.VMEM((3, n_line) + message, F32),
            pltpu.VMEM((3, n_line, 1, own), F32),
            pltpu.VMEM((2, n_line, 2 * cols, own), F32),
            pltpu.VMEM((3, n_plane) + message, F32),
            pltpu.VMEM((3, n_plane, 1, own), F32),
            pltpu.VMEM((2, n_plane) + message, F32),
            pltpu.VMEM((n_plane, 1, own), F32),
            pltpu.VMEM((2 * (n_plane - 1),) + message, F32),
            pltpu.VMEM((n_plane // 2, n_line * own, 4 * own), BF16),
            pltpu.SemaphoreType.DMA((7,)),
            pltpu.SemaphoreType.DMA((20,)),
            pltpu.SemaphoreType.DMA((20,)),
        ],
        compiler_params=pltpu.CompilerParams(
            collective_id=0, has_side_effects=True, vmem_limit_bytes=62 * 1024 * 1024
        ),
    )(
        points,
        inverse_length.reshape(1, dim),
        target.reshape(1, own),
        probe_bits,
        leaf_inverse,
        top_basis,
        sub_basis,
    )


def solution(mesh):
    return jax.shard_map(
        functools.partial(on_device, mesh.shape["row"], mesh.shape["col"]),
        mesh=mesh,
        in_specs=(
            P(None, ("row", "col")),
            P(),
            P(("row", "col")),
            P(None, ("row", "col")),
            P(("row", "col"), None),
            P(None, ("row", "col")),
            P(None, ("row", "col")),
        ),
        out_specs=(P(None, ("row", "col")), P(None, ("row", "col")), P()),
        check_vma=False,
    )
```

time: 43.3 us -> 42.7 us (0.986)
  Pallas kernels: 39.8 us -> 39.2 us
    pallas_call x1, Pallas kernels: 39.8 us -> 39.2 us  [on_device(): pl.pallas_call(functools.partial(kernel, n_row, n_col, low, rank), out_sh...]
where the time goes in v2:
time: 42.7 us; the launch traced here: 42.4 us
  Pallas kernels  39.2 us (92%)
  local copies, waits for them, and re-layouts  2.55 us (6%)
  between operations  0.65 us (2%)
    pallas_call x1, Pallas kernels, on_device(): pl.pallas_call(functools.partial(kernel, n_row, n_col, low, rank), out_sh...  39.2 us
    unnamed x7, local copies, waits for them, and re-layouts  2.55 us

profile of v2, /device:TPU:0, one launch (start us, length us, event | category | flops | bytes accessed | tf_op | source)
XLA Modules:
  0.0 42.4 jit_solution(2468285993306094993)
XLA Ops:
  0.6 39.2 %shard_map.94 = (f32[16,128]{1,0:T(8,128)}, f32[16,128]{1,0:T(8,128)}, f32[2,2,16]{2,1,0:T(2,128)}) custom-call(f32[16,128]{1,0:T(8,128)} %points_hbm.1, f32[1,16]{1,0:T(1,128)} %bitcast.2, f32[1,128]{1,0:T(1,128)} %bitcast.3, s32[15,128]{1,0:T(8,128)} %bits_hbm.1, f32[128,128]{1,0:T(8,128)} %leaf_hbm.1, f32[64,128]{1,0:T(8,128)} %top_hbm.1, f32[64,128]{1,0:T(8,128)} %sub_hbm.1), custom_call_target="tpu_custom_call" | custom-call | tf_op jit(solution)/shard_map/pallas_call | solution.py:413
  39.8 0.0 copy-start
  39.8 1.3 %copy.13 = f32[16,128]{1,0:T(8,128)} copy(f32[16,128]{1,0:T(8,128)} %get-tuple-element.6) | data formatting | bytes 16384
  41.1 0.0 copy-done
  41.1 0.0 copy-start.1
  41.1 0.6 %copy.14 = f32[16,128]{1,0:T(8,128)} copy(f32[16,128]{1,0:T(8,128)S(1)} %copy-done) | data formatting | bytes 16384
  41.7 0.1 copy-done.1
  41.8 0.6 %copy.15 = f32[2,2,16]{2,1,0:T(2,128)} copy(f32[2,2,16]{2,1,0:T(2,128)S(1)} %copy-done.1) | data formatting | bytes 512
Async XLA Ops:
  39.8 1.3 %copy-start = (f32[16,128]{1,0:T(8,128)S(1)}, f32[16,128]{1,0:T(8,128)}, u32[]{:S(2)}) copy-start(f32[16,128]{1,0:T(8,128)} %get-tuple-element.7) | copy-start | bytes 24580
  41.1 0.7 %copy-start.1 = (f32[2,2,16]{2,1,0:T(2,128)S(1)}, f32[2,2,16]{2,1,0:T(2,128)}, u32[]{:S(2)}) copy-start(f32[2,2,16]{2,1,0:T(2,128)} %get-tuple-element.8) | copy-start | bytes 772

commit v3 on v2

--- a/solution.py
+++ b/solution.py
@@ -33,10 +33,6 @@
     return lax.dot_general(a, b, (((1,), (0,)), ((), ())), preferred_element_type=F32)
 
 
-def dot_nt(a, b):
-    return lax.dot_general(a, b, (((1,), (1,)), ((), ())), preferred_element_type=F32)
-
-
 def fold(out):
     rows, width = out.shape[0] // 2, out.shape[1] // 2
     return (
@@ -46,6 +42,10 @@
 
 def stacked(x):
     return jnp.concatenate(halves(x), axis=0)
+
+
+def beside(x):
+    return jnp.concatenate(halves(x), axis=1)
 
 
 def kernel(
@@ -87,18 +87,19 @@
     recv_sem,
 ):
     n_high = n_col // low
-    n_line, n_plane = low, n_row * n_high
+    n_line, n_plane = n_high, n_row * low
     row, col = lax.axis_index("row"), lax.axis_index("col")
     high = lax.div(col, low)
-    in_line = lax.rem(col, low)
-    in_plane = row * n_high + high
+    lowest = lax.rem(col, low)
+    in_line = high
+    in_plane = row * low + lowest
     cols, own = rhs_ref.shape
     dim = points_ref.shape[0]
 
-    line_peers = [(row, high * low + lax.rem(in_line + t, n_line)) for t in range(1, n_line)]
+    line_peers = [(row, lax.rem(in_line + t, n_line) * low + lowest) for t in range(1, n_line)]
     plane_slots = [lax.rem(in_plane + t, n_plane) for t in range(n_plane)]
     plane_peers = [
-        (lax.div(slot, n_high), lax.rem(slot, n_high) * low + in_line) for slot in plane_slots[1:]
+        (lax.div(slot, low), in_line * low + lax.rem(slot, low)) for slot in plane_slots[1:]
     ]
 
     loads = [
@@ -187,17 +188,17 @@
     pts_plane_ref[in_plane] = scaled
     for load in loads[4:]:
         load.wait()
-    basis_tall = stacked(basis_ref[in_line])
-    leaf_tall = stacked(leaf_ref[...])
+    basis_wide = beside(basis_ref[in_line].T)
+    leaf_wide = beside(leaf_ref[...])
 
     def project(v):
-        return fold(dot_nt(stacked(v), basis_tall))
+        return fold(dot_nn(stacked(v), basis_wide))
 
     def expand(c):
         return fold(dot_nn(stacked(c), wide_ref[...]))
 
     def leaf(v):
-        return fold(dot_nt(stacked(v), leaf_tall))
+        return fold(dot_nn(stacked(v), leaf_wide))
 
     def total(buf, first, count):
         out = buf[first]
@@ -228,7 +229,7 @@
 
     def by_subtree(at):
         all_plane(plane_ref.at[at], 4 * at + 2).wait_recv()
-        return [total(plane_ref.at[at], i * n_high, n_high) for i in range(n_row)]
+        return [total(plane_ref.at[at], i * low, low) for i in range(n_row)]
 
     def all_stats(at):
         all_plane(plane_stat_ref.at[at], 4 * at + 3).wait_recv()
@@ -403,7 +404,7 @@
 
 def on_device(n_row, n_col, points, inverse_length, target, probe_bits, leaf_inverse, top_basis, sub_basis):
     low = math.gcd(n_col, 4)
-    n_line, n_plane = low, n_row * (n_col // low)
+    n_line, n_plane = n_col // low, n_row * low
     dim, own = points.shape
     cols = probe_bits.shape[0] + 1
     rank = top_basis.shape[0]

time: 42.7 us -> 43.5 us (1.019)
  Pallas kernels: 39.2 us -> 40 us
    pallas_call x1, Pallas kernels: 39.2 us -> 40 us  [on_device(): pl.pallas_call(functools.partial(kernel, n_row, n_col, low, rank), out_sh...]
where the time goes in v3:
time: 43.5 us; the launch traced here: 43.2 us
  Pallas kernels  40 us (92%)
  local copies, waits for them, and re-layouts  2.55 us (6%)
  between operations  0.65 us (1%)
    pallas_call x1, Pallas kernels, on_device(): pl.pallas_call(functools.partial(kernel, n_row, n_col, low, rank), out_sh...  40 us
    unnamed x7, local copies, waits for them, and re-layouts  2.55 us

profile of v3, /device:TPU:0, one launch (start us, length us, event | category | flops | bytes accessed | tf_op | source)
XLA Modules:
  0.0 43.2 jit_solution(4345866162292173308)
XLA Ops:
  0.6 40.0 %shard_map.94 = (f32[16,128]{1,0:T(8,128)}, f32[16,128]{1,0:T(8,128)}, f32[2,2,16]{2,1,0:T(2,128)}) custom-call(f32[16,128]{1,0:T(8,128)} %points_hbm.1, f32[1,16]{1,0:T(1,128)} %bitcast.2, f32[1,128]{1,0:T(1,128)} %bitcast.3, s32[15,128]{1,0:T(8,128)} %bits_hbm.1, f32[128,128]{1,0:T(8,128)} %leaf_hbm.1, f32[64,128]{1,0:T(8,128)} %top_hbm.1, f32[64,128]{1,0:T(8,128)} %sub_hbm.1), custom_call_target="tpu_custom_call" | custom-call | tf_op jit(solution)/shard_map/pallas_call | solution.py:414
  40.6 0.0 copy-start
  40.6 1.3 %copy.13 = f32[16,128]{1,0:T(8,128)} copy(f32[16,128]{1,0:T(8,128)} %get-tuple-element.6) | data formatting | bytes 16384
  41.9 0.0 copy-done
  41.9 0.0 copy-start.1
  41.9 0.6 %copy.14 = f32[16,128]{1,0:T(8,128)} copy(f32[16,128]{1,0:T(8,128)S(1)} %copy-done) | data formatting | bytes 16384
  42.5 0.1 copy-done.1
  42.6 0.6 %copy.15 = f32[2,2,16]{2,1,0:T(2,128)} copy(f32[2,2,16]{2,1,0:T(2,128)S(1)} %copy-done.1) | data formatting | bytes 512
Async XLA Ops:
  40.6 1.3 %copy-start = (f32[16,128]{1,0:T(8,128)S(1)}, f32[16,128]{1,0:T(8,128)}, u32[]{:S(2)}) copy-start(f32[16,128]{1,0:T(8,128)} %get-tuple-element.7) | copy-start | bytes 24580
  41.9 0.7 %copy-start.1 = (f32[2,2,16]{2,1,0:T(2,128)S(1)}, f32[2,2,16]{2,1,0:T(2,128)}, u32[]{:S(2)}) copy-start(f32[2,2,16]{2,1,0:T(2,128)} %get-tuple-element.8) | copy-start | bytes 772

commit v4 on v2

--- a/solution.py
+++ b/solution.py
@@ -33,10 +33,6 @@
     return lax.dot_general(a, b, (((1,), (0,)), ((), ())), preferred_element_type=F32)
 
 
-def dot_nt(a, b):
-    return lax.dot_general(a, b, (((1,), (1,)), ((), ())), preferred_element_type=F32)
-
-
 def fold(out):
     rows, width = out.shape[0] // 2, out.shape[1] // 2
     return (
@@ -46,6 +42,10 @@
 
 def stacked(x):
     return jnp.concatenate(halves(x), axis=0)
+
+
+def beside(x):
+    return jnp.concatenate(halves(x), axis=1)
 
 
 def kernel(
@@ -74,13 +74,12 @@
     pts_line_ref,
     pts_plane_ref,
     line_ref,
-    line_stat_ref,
     extra_ref,
     plane_ref,
-    plane_stat_ref,
     prod_ref,
     prod_stat_ref,
     out_ref,
+    out_stat_ref,
     kmat_ref,
     load_sem,
     send_sem,
@@ -187,17 +186,17 @@
     pts_plane_ref[in_plane] = scaled
     for load in loads[4:]:
         load.wait()
-    basis_tall = stacked(basis_ref[in_line])
-    leaf_tall = stacked(leaf_ref[...])
+    basis_wide = beside(basis_ref[in_line].T)
+    leaf_wide = beside(leaf_ref[...])
 
     def project(v):
-        return fold(dot_nt(stacked(v), basis_tall))
+        return fold(dot_nn(stacked(v), basis_wide))
 
     def expand(c):
         return fold(dot_nn(stacked(c), wide_ref[...]))
 
     def leaf(v):
-        return fold(dot_nt(stacked(v), leaf_tall))
+        return fold(dot_nn(stacked(v), leaf_wide))
 
     def total(buf, first, count):
         out = buf[first]
@@ -205,34 +204,24 @@
             out = out + buf[i]
         return out
 
-    def send_coef(at, vector):
-        line_ref[at, in_line] = project(vector)
-        send_line(line_ref.at[at], 4 * at)
-
-    def send_stat(at, *columns):
-        line_stat_ref[at, in_line] = to_row(*columns)
-        send_line(line_stat_ref.at[at], 4 * at + 1)
+    def put(at, vector, *columns):
+        line_ref[at, in_line, 0:cols, :] = project(vector)
+        line_ref[at, in_line, cols : cols + 1, :] = to_row(*columns)
 
     def send_extra(at, *more):
         for i, part in enumerate(more):
             extra_ref[at, in_line, i * cols : (i + 1) * cols, :] = part
-        send_line(extra_ref.at[at], 12 + at)
+        send_line(extra_ref.at[at], 6 + at)
 
     def cross(at):
-        all_line(line_ref.at[at], 4 * at).wait_recv()
+        all_line(line_ref.at[at], at).wait_recv()
         plane_ref[at, in_plane] = total(line_ref.at[at], 0, n_line)
-        send_plane(plane_ref.at[at], 4 * at + 2)
-        all_line(line_stat_ref.at[at], 4 * at + 1).wait_recv()
-        plane_stat_ref[at, in_plane] = total(line_stat_ref.at[at], 0, n_line)
-        send_plane(plane_stat_ref.at[at], 4 * at + 3)
+        send_plane(plane_ref.at[at], 3 + at)
 
     def by_subtree(at):
-        all_plane(plane_ref.at[at], 4 * at + 2).wait_recv()
-        return [total(plane_ref.at[at], i * n_high, n_high) for i in range(n_row)]
-
-    def all_stats(at):
-        all_plane(plane_stat_ref.at[at], 4 * at + 3).wait_recv()
-        return total(plane_stat_ref.at[at], 0, n_plane)
+        all_plane(plane_ref.at[at], 3 + at).wait_recv()
+        sums = [total(plane_ref.at[at], i * n_high, n_high) for i in range(n_row)]
+        return [s[0:cols] for s in sums], sum([s[cols:] for s in sums[1:]], sums[0][cols:])
 
     def of_line(at, which):
         rows = slice(which * cols, (which + 1) * cols)
@@ -257,16 +246,14 @@
             squares = squares + jnp.where(is_top, 0.0, part * part)
         return jnp.sum(squares, axis=1, keepdims=True)
 
-    line_ref[0, in_line] = project(rhs)
     leaf_res = leaf(rhs)
-    line_stat_ref[0, in_line] = to_row(dots(rhs, leaf_res))
+    put(0, rhs, dots(rhs, leaf_res))
     pl.semaphore_wait(barrier, n_line + n_plane - 2)
     send_line(line_ref.at[0], 0)
-    send_line(line_stat_ref.at[0], 1)
-    send_line(pts_line_ref, 14)
-    send_plane(pts_plane_ref, 15)
+    send_line(pts_line_ref, 8)
+    send_plane(pts_plane_ref, 9)
     send_extra(0, leaf_res, rhs)
-    send_line(basis_ref, 16)
+    send_line(basis_ref, 10)
 
     def norm_rows(sq, first):
         pieces = [p.astype(F32) for p in thirds(sq)]
@@ -281,14 +268,14 @@
         sq = jnp.sum(x * x, axis=0, keepdims=True)
         return [pieces[at] for at in order], norm_rows(sq, first)
 
-    all_line(pts_line_ref, 14).wait_recv()
+    all_line(pts_line_ref, 8).wait_recv()
     sources = jnp.concatenate([pts_line_ref[i] for i in range(n_line)], axis=1)
     src_parts, src_norm = features(sources, (0, 0, 0, 1, 1, 2), 0)
     src_feat = jnp.concatenate(
         [-2.0 * p.astype(F32) for p in src_parts] + [src_norm.astype(F32)], axis=0
     ).T.astype(BF16)
     cross(0)
-    all_plane(pts_plane_ref, 15).wait_recv()
+    all_plane(pts_plane_ref, 9).wait_recv()
 
     def build(q, carry):
         pair = jnp.concatenate(
@@ -308,97 +295,91 @@
 
     lax.fori_loop(0, n_plane // 2, build, 0)
 
-    all_line(basis_ref, 16).wait_recv()
+    all_line(basis_ref, 10).wait_recv()
     for i in range(n_line):
         hi, lo = halves(basis_ref[i])
         wide_ref[:, i * own : (i + 1) * own] = hi
         wide_ref[:, (n_line + i) * own : (n_line + i + 1) * own] = lo
 
-    def send_products(which, vectors):
+    def send_products(inbox, outbox, at, vectors, line):
         mine = stacked(vectors)
         for q in range(n_plane // 2):
             both = fold(dot_nn(mine, kmat_ref[q]))
             for half in range(2):
                 t = 2 * q + 1 + half
                 block = both[:, half * own : (half + 1) * own]
-                if t == n_plane:
-                    prod_ref[which, in_plane] = block
-                    continue
-                slot = which * (n_plane - 1) + t - 1
-                out_ref[slot] = block
-                remote(
-                    out_ref.at[slot], prod_ref.at[which, in_plane], 17 + which, plane_peers[t - 1]
-                ).start()
-
-    def products(which):
-        all_plane(prod_ref.at[which], 17 + which).wait_recv()
-        return total(prod_ref.at[which], 0, n_plane)
-
-    all_line(extra_ref.at[0], 12).wait_recv()
+                slot, where = (inbox, in_plane) if t == n_plane else (outbox, t - 1)
+                slot[where, 0:cols, :] = block
+                if line is not None:
+                    slot[where, cols : cols + 1, :] = line
+                if t < n_plane:
+                    remote(outbox.at[where], inbox.at[in_plane], at, plane_peers[t - 1]).start()
+
+    def products(inbox, at):
+        all_plane(inbox, at).wait_recv()
+        return total(inbox, 0, n_plane)
+
+    all_line(extra_ref.at[0], 6).wait_recv()
     leaf_lanes = of_line(0, 0)
-    parts = by_subtree(0)
+    parts, stat = by_subtree(0)
     lanes = leaf_lanes + expand(own_coef(parts))
-    send_products(0, lanes)
+    send_products(prod_ref, out_ref, 11, lanes, None)
     direction = pick(lanes)
-    rz_now = to_col(all_stats(0)) + level_product(parts)
-
-    image = products(0) + noise_level * direction
-    send_coef(1, image)
-    send_stat(1, dots(direction, image))
+    rz_now = to_col(stat) + level_product(parts)
+
+    image = products(prod_ref, 11) + noise_level * direction
+    put(1, image, dots(direction, image))
+    send_line(line_ref.at[1], 1)
     leaf_image = leaf(image)
     send_extra(1, leaf_image, image)
     cross(1)
-    all_line(extra_ref.at[1], 13).wait_recv()
+    all_line(extra_ref.at[1], 7).wait_recv()
     leaf_step = of_line(1, 0)
-    alpha_0 = rz_now / to_col(all_stats(1))
-    sums = by_subtree(1)
+    sums, stat = by_subtree(1)
+    alpha_0 = rz_now / to_col(stat)
     parts = [a - alpha_0 * s for a, s in zip(parts, sums)]
     leaf_lanes = leaf_lanes - alpha_0 * leaf_step
+    residual_lanes = of_line(0, 1) - alpha_0 * of_line(1, 1)
+    leaf_line = to_row(dots(residual_lanes, leaf_lanes))
     lanes = leaf_lanes + expand(own_coef(parts))
-    send_products(1, lanes)
-    residual_lanes = of_line(0, 1) - alpha_0 * of_line(1, 1)
-    prod_stat_ref[in_plane] = to_row(dots(residual_lanes, leaf_lanes))
-    send_plane(prod_stat_ref, 19)
+    send_products(prod_stat_ref, out_stat_ref, 12, lanes, leaf_line)
     answer = alpha_0 * direction
     residual = rhs - alpha_0 * image
     leaf_res = leaf_res - alpha_0 * leaf_image
     precond = pick(lanes)
     levels = level_product(parts)
 
-    all_plane(prod_stat_ref, 19).wait_recv()
-    leaf_total = to_col(total(prod_stat_ref, 0, n_plane))
+    product = products(prod_stat_ref, 12)
+    leaf_total = to_col(product[cols:])
     rz_next = leaf_total + levels
     beta_0 = rz_next / rz_now
     rz_now = rz_next
     direction = precond + beta_0 * direction
-    rest = noise_level * precond + beta_0 * image
-    image = products(1) + rest
-    send_coef(2, image)
+    image = product[0:cols] + noise_level * precond + beta_0 * image
     leaf_image = leaf(image)
-    send_stat(2, dots(direction, image), dots(image, leaf_res), dots(image, leaf_image))
+    put(2, image, dots(direction, image), dots(image, leaf_res), dots(image, leaf_image))
+    send_line(line_ref.at[2], 2)
     cross(2)
-    stat = all_stats(2)
+    sums, stat = by_subtree(2)
     alpha_1 = rz_now / to_col(stat)
     sol_ref[...] = answer + alpha_1 * direction
     res_ref[...] = residual - alpha_1 * image
     leaf_last = leaf_total - alpha_1 * (2.0 * to_col(stat, 1) - alpha_1 * to_col(stat, 2))
-    parts = [a - alpha_1 * s for a, s in zip(parts, by_subtree(2))]
+    parts = [a - alpha_1 * s for a, s in zip(parts, sums)]
     beta_1 = (leaf_last + level_product(parts)) / rz_now
     for i, (alpha, beta) in enumerate(((alpha_0, beta_0), (alpha_1, beta_1))):
         coef_ref[0, i : i + 1, :] = to_row(alpha)[:, 0:cols]
         coef_ref[1, i : i + 1, :] = to_row(beta)[:, 0:cols]
     for at in range(3):
-        all_line(line_ref.at[at], 4 * at).wait_send()
-        all_line(line_stat_ref.at[at], 4 * at + 1).wait_send()
-        all_plane(plane_ref.at[at], 4 * at + 2).wait_send()
-        all_plane(plane_stat_ref.at[at], 4 * at + 3).wait_send()
+        all_line(line_ref.at[at], at).wait_send()
+        all_plane(plane_ref.at[at], 3 + at).wait_send()
     for at in range(2):
-        all_line(extra_ref.at[at], 12 + at).wait_send()
-        all_plane(prod_ref.at[at], 17 + at).wait_send()
-    all_line(pts_line_ref, 14).wait_send()
-    all_plane(pts_plane_ref, 15).wait_send()
-    all_line(basis_ref, 16).wait_send()
-    all_plane(prod_stat_ref, 19).wait_send()
+        all_line(extra_ref.at[at], 6 + at).wait_send()
+    all_line(pts_line_ref, 8).wait_send()
+    all_plane(pts_plane_ref, 9).wait_send()
+    all_line(basis_ref, 10).wait_send()
+    all_plane(prod_ref, 11).wait_send()
+    all_plane(prod_stat_ref, 12).wait_send()
 
 
 def on_device(n_row, n_col, points, inverse_length, target, probe_bits, leaf_inverse, top_basis, sub_basis):
@@ -409,7 +390,6 @@
     rank = top_basis.shape[0]
     vmem = pl.BlockSpec(memory_space=pltpu.VMEM)
     hbm = pl.BlockSpec(memory_space=pltpu.HBM)
-    message = (cols, own)
     return pl.pallas_call(
         functools.partial(kernel, n_row, n_col, low, rank),
         out_shape=(
@@ -430,18 +410,17 @@
             pltpu.VMEM((cols, own), F32),
             pltpu.VMEM((n_line, dim, own), F32),
             pltpu.VMEM((n_plane, dim, own), F32),
-            pltpu.VMEM((3, n_line) + message, F32),
-            pltpu.VMEM((3, n_line, 1, own), F32),
+            pltpu.VMEM((3, n_line, cols + 1, own), F32),
             pltpu.VMEM((2, n_line, 2 * cols, own), F32),
-            pltpu.VMEM((3, n_plane) + message, F32),
-            pltpu.VMEM((3, n_plane, 1, own), F32),
-            pltpu.VMEM((2, n_plane) + message, F32),
-            pltpu.VMEM((n_plane, 1, own), F32),
-            pltpu.VMEM((2 * (n_plane - 1),) + message, F32),
+            pltpu.VMEM((3, n_plane, cols + 1, own), F32),
+            pltpu.VMEM((n_plane, cols, own), F32),
+            pltpu.VMEM((n_plane, cols + 1, own), F32),
+            pltpu.VMEM((n_plane - 1, cols, own), F32),
+            pltpu.VMEM((n_plane - 1, cols + 1, own), F32),
             pltpu.VMEM((n_plane // 2, n_line * own, 4 * own), BF16),
             pltpu.SemaphoreType.DMA((7,)),
-            pltpu.SemaphoreType.DMA((20,)),
-            pltpu.SemaphoreType.DMA((20,)),
+            pltpu.SemaphoreType.DMA((13,)),
+            pltpu.SemaphoreType.DMA((13,)),
         ],
         compiler_params=pltpu.CompilerParams(
             collective_id=0, has_side_effects=True, vmem_limit_bytes=62 * 1024 * 1024

time: 42.7 us -> 41.7 us (0.977)
  Pallas kernels: 39.2 us -> 38.2 us
    pallas_call x1, Pallas kernels: 39.2 us -> 38.2 us  [on_device(): pl.pallas_call(functools.partial(kernel, n_row, n_col, low, rank), out_sh...]
where the time goes in v4:
time: 41.7 us; the launch traced here: 41.4 us
  Pallas kernels  38.2 us (92%)
  local copies, waits for them, and re-layouts  2.55 us (6%)
  between operations  0.65 us (2%)
    pallas_call x1, Pallas kernels, on_device(): pl.pallas_call(functools.partial(kernel, n_row, n_col, low, rank), out_sh...  38.2 us
    unnamed x7, local copies, waits for them, and re-layouts  2.55 us

profile of v4, /device:TPU:0, one launch (start us, length us, event | category | flops | bytes accessed | tf_op | source)
XLA Modules:
  0.0 41.4 jit_solution(15165138656987075815)
XLA Ops:
  0.6 38.2 %shard_map.94 = (f32[16,128]{1,0:T(8,128)}, f32[16,128]{1,0:T(8,128)}, f32[2,2,16]{2,1,0:T(2,128)}) custom-call(f32[16,128]{1,0:T(8,128)} %points_hbm.1, f32[1,16]{1,0:T(1,128)} %bitcast.2, f32[1,128]{1,0:T(1,128)} %bitcast.3, s32[15,128]{1,0:T(8,128)} %bits_hbm.1, f32[128,128]{1,0:T(8,128)} %leaf_hbm.1, f32[64,128]{1,0:T(8,128)} %top_hbm.1, f32[64,128]{1,0:T(8,128)} %sub_hbm.1), custom_call_target="tpu_custom_call" | custom-call | tf_op jit(solution)/shard_map/pallas_call | solution.py:393
  38.8 0.0 copy-start
  38.8 1.3 %copy.13 = f32[16,128]{1,0:T(8,128)} copy(f32[16,128]{1,0:T(8,128)} %get-tuple-element.6) | data formatting | bytes 16384
  40.1 0.0 copy-done
  40.1 0.0 copy-start.1
  40.1 0.6 %copy.14 = f32[16,128]{1,0:T(8,128)} copy(f32[16,128]{1,0:T(8,128)S(1)} %copy-done) | data formatting | bytes 16384
  40.7 0.1 copy-done.1
  40.8 0.6 %copy.15 = f32[2,2,16]{2,1,0:T(2,128)} copy(f32[2,2,16]{2,1,0:T(2,128)S(1)} %copy-done.1) | data formatting | bytes 512
Async XLA Ops:
  38.8 1.3 %copy-start = (f32[16,128]{1,0:T(8,128)S(1)}, f32[16,128]{1,0:T(8,128)}, u32[]{:S(2)}) copy-start(f32[16,128]{1,0:T(8,128)} %get-tuple-element.7) | copy-start | bytes 24580
  40.1 0.7 %copy-start.1 = (f32[2,2,16]{2,1,0:T(2,128)S(1)}, f32[2,2,16]{2,1,0:T(2,128)}, u32[]{:S(2)}) copy-start(f32[2,2,16]{2,1,0:T(2,128)} %get-tuple-element.8) | copy-start | bytes 772

commit v5 on v4

--- a/solution.py
+++ b/solution.py
@@ -13,7 +13,6 @@
 F32 = jnp.float32
 BF16 = jnp.bfloat16
 
-root_five = math.sqrt(5.0)
 noise_level = 0.5
 
 
@@ -287,7 +286,7 @@
             some = src_feat[i * own : (i + 1) * own]
             five_sq = jnp.maximum(5.0 * dot_nn(some, far_feat), 1e-30)
             dist = five_sq * lax.rsqrt(five_sq)
-            value = (1.0 + dist + five_sq * (1.0 / 3.0)) * jnp.exp(-dist)
+            value = (1.0 + dist + five_sq * (1.0 / 3.0)) * jnp.exp2(dist * (-1.0 / math.log(2.0)))
             hi, lo = halves(value)
             kmat_ref[q, i * own : (i + 1) * own, 0 : 2 * own] = hi
             kmat_ref[q, i * own : (i + 1) * own, 2 * own :] = lo
@@ -423,7 +422,7 @@
             pltpu.SemaphoreType.DMA((13,)),
         ],
         compiler_params=pltpu.CompilerParams(
-            collective_id=0, has_side_effects=True, vmem_limit_bytes=62 * 1024 * 1024
+            collective_id=0, has_side_effects=True, vmem_limit_bytes=55202 * 1024
         ),
     )(
         points,

time: 41.7 us -> 40.8 us (0.978)
  Pallas kernels: 38.2 us -> 37.5 us
    pallas_call x1, Pallas kernels: 38.2 us -> 37.5 us  [on_device(): pl.pallas_call(functools.partial(kernel, n_row, n_col, low, rank), out_sh...]
where the time goes in v5:
time: 40.8 us; the launch traced here: 40.6 us
  Pallas kernels  37.5 us (92%)
  local copies, waits for them, and re-layouts  2.43 us (6%)
  between operations  0.66 us (2%)
    pallas_call x1, Pallas kernels, on_device(): pl.pallas_call(functools.partial(kernel, n_row, n_col, low, rank), out_sh...  37.5 us
    unnamed x7, local copies, waits for them, and re-layouts  2.43 us

profile of v5, /device:TPU:0, one launch (start us, length us, event | category | flops | bytes accessed | tf_op | source)
XLA Modules:
  0.0 40.6 jit_solution(15767149158592187619)
XLA Ops:
  0.6 0.0 copy-start
  0.6 0.0 copy-start.1
  0.7 0.6 %copy-done = f32[16]{0:T(128)S(1)} copy-done((f32[16]{0:T(128)S(1)}, f32[16]{0:T(128)}, u32[]{:S(2)}) %copy-start) | copy-done | bytes 88
  1.3 0.0 copy-done.1
  1.3 37.5 %shard_map.94 = (f32[16,128]{1,0:T(8,128)S(1)}, f32[16,128]{1,0:T(8,128)S(1)}, f32[2,2,16]{2,1,0:T(2,128)S(1)}) custom-call(f32[16,128]{1,0:T(8,128)} %points_hbm.1, f32[1,16]{1,0:T(1,128)S(1)} %bitcast.2, f32[1,128]{1,0:T(1,128)S(1)} %bitcast.3, s32[15,128]{1,0:T(8,128)} %bits_hbm.1, f32[128,128]{1,0:T(8,128)} %leaf_hbm.1, f32[64,128]{1,0:T(8,128)} %top_hbm.1, ...), custom_call_target="tpu_custom_call" | custom-call | tf_op jit(solution)/shard_map/pallas_call | solution.py:392
  38.8 0.6 %copy.13 = f32[16,128]{1,0:T(8,128)} copy(f32[16,128]{1,0:T(8,128)S(1)} %get-tuple-element.6) | data formatting | bytes 16384
  39.4 0.6 %copy.14 = f32[16,128]{1,0:T(8,128)} copy(f32[16,128]{1,0:T(8,128)S(1)} %get-tuple-element.7) | data formatting | bytes 16384
  40.0 0.6 %copy.15 = f32[2,2,16]{2,1,0:T(2,128)} copy(f32[2,2,16]{2,1,0:T(2,128)S(1)} %get-tuple-element.8) | data formatting | bytes 512
Async XLA Ops:
  0.6 0.7 %copy-start = (f32[16]{0:T(128)S(1)}, f32[16]{0:T(128)}, u32[]{:S(2)}) copy-start(f32[16]{0:T(128)} %param.8) | copy-start | bytes 196
  0.6 0.7 %copy-start.1 = (f32[128]{0:T(128)S(1)}, f32[128]{0:T(128)}, u32[]{:S(2)}) copy-start(f32[128]{0:T(128)} %param.9) | copy-start | bytes 1540

commit v6 on v5

--- a/solution.py
+++ b/solution.py
@@ -83,6 +83,7 @@
     load_sem,
     send_sem,
     recv_sem,
+    pts_sem,
 ):
     n_high = n_col // low
     n_line, n_plane = low, n_row * n_high
@@ -98,6 +99,10 @@
     plane_peers = [
         (lax.div(slot, n_high), lax.rem(slot, n_high) * low + in_line) for slot in plane_slots[1:]
     ]
+
+    barrier = pltpu.get_barrier_semaphore()
+    for peer in line_peers + plane_peers:
+        pl.semaphore_signal(barrier, inc=1, device_id=peer, device_id_type=MESH)
 
     loads = [
         pltpu.make_async_copy(src, dst, load_sem.at[at])
@@ -115,10 +120,6 @@
     ]
     for load in loads:
         load.start()
-
-    barrier = pltpu.get_barrier_semaphore()
-    for peer in line_peers + plane_peers:
-        pl.semaphore_signal(barrier, inc=1, device_id=peer, device_id_type=MESH)
 
     def remote(src, dst, at, device):
         return pltpu.make_async_remote_copy(
@@ -245,14 +246,26 @@
             squares = squares + jnp.where(is_top, 0.0, part * part)
         return jnp.sum(squares, axis=1, keepdims=True)
 
+    def points_to(t, peer):
+        return pltpu.make_async_remote_copy(
+            src_ref=pts_plane_ref.at[in_plane],
+            dst_ref=pts_plane_ref.at[in_plane],
+            send_sem=send_sem.at[9],
+            recv_sem=pts_sem.at[t],
+            device_id=peer,
+            device_id_type=MESH,
+        )
+
     leaf_res = leaf(rhs)
     put(0, rhs, dots(rhs, leaf_res))
     pl.semaphore_wait(barrier, n_line + n_plane - 2)
     send_line(line_ref.at[0], 0)
     send_line(pts_line_ref, 8)
-    send_plane(pts_plane_ref, 9)
+    for t, peer in enumerate(plane_peers, 1):
+        points_to(t, peer).start()
     send_extra(0, leaf_res, rhs)
     send_line(basis_ref, 10)
+    cross(0)
 
     def norm_rows(sq, first):
         pieces = [p.astype(F32) for p in thirds(sq)]
@@ -273,10 +286,10 @@
     src_feat = jnp.concatenate(
         [-2.0 * p.astype(F32) for p in src_parts] + [src_norm.astype(F32)], axis=0
     ).T.astype(BF16)
-    cross(0)
-    all_plane(pts_plane_ref, 9).wait_recv()
-
-    def build(q, carry):
+
+    def build(q, carry, arriving=2):
+        for i in range(arriving):
+            points_to(n_plane - 1 - 2 * q - i, plane_peers[0]).wait_recv()
         pair = jnp.concatenate(
             [pts_plane_ref[lax.rem(in_plane + 2 * q + i, n_plane)] for i in (1, 2)], axis=1
         )
@@ -292,7 +305,8 @@
             kmat_ref[q, i * own : (i + 1) * own, 2 * own :] = lo
         return carry
 
-    lax.fori_loop(0, n_plane // 2, build, 0)
+    lax.fori_loop(0, n_plane // 2 - 1, build, 0)
+    build(n_plane // 2 - 1, 0, 1)
 
     all_line(basis_ref, 10).wait_recv()
     for i in range(n_line):
@@ -420,6 +434,7 @@
             pltpu.SemaphoreType.DMA((7,)),
             pltpu.SemaphoreType.DMA((13,)),
             pltpu.SemaphoreType.DMA((13,)),
+            pltpu.SemaphoreType.DMA((n_plane,)),
         ],
         compiler_params=pltpu.CompilerParams(
             collective_id=0, has_side_effects=True, vmem_limit_bytes=55202 * 1024

time: 40.8 us -> 40.4 us (level)
    pallas_call x1, Pallas kernels: 37.5 us -> 37.1 us  [on_device(): pl.pallas_call(functools.partial(kernel, n_row, n_col, low, rank), out_sh...]
where the time goes in v6:
time: 40.4 us; the launch traced here: 40.2 us
  Pallas kernels  37.1 us (92%)
  local copies, waits for them, and re-layouts  2.43 us (6%)
  between operations  0.66 us (2%)
    pallas_call x1, Pallas kernels, on_device(): pl.pallas_call(functools.partial(kernel, n_row, n_col, low, rank), out_sh...  37.1 us
    unnamed x7, local copies, waits for them, and re-layouts  2.43 us

profile of v6, /device:TPU:0, one launch (start us, length us, event | category | flops | bytes accessed | tf_op | source)
XLA Modules:
  0.0 40.2 jit_solution(4972927933297868349)
XLA Ops:
  0.6 0.0 copy-start
  0.6 0.0 copy-start.1
  0.7 0.6 %copy-done = f32[16]{0:T(128)S(1)} copy-done((f32[16]{0:T(128)S(1)}, f32[16]{0:T(128)}, u32[]{:S(2)}) %copy-start) | copy-done | bytes 88
  1.3 0.0 copy-done.1
  1.3 37.1 %shard_map.94 = (f32[16,128]{1,0:T(8,128)S(1)}, f32[16,128]{1,0:T(8,128)S(1)}, f32[2,2,16]{2,1,0:T(2,128)S(1)}) custom-call(f32[16,128]{1,0:T(8,128)} %points_hbm.1, f32[1,16]{1,0:T(1,128)S(1)} %bitcast.2, f32[1,128]{1,0:T(1,128)S(1)} %bitcast.3, s32[15,128]{1,0:T(8,128)} %bits_hbm.1, f32[128,128]{1,0:T(8,128)} %leaf_hbm.1, f32[64,128]{1,0:T(8,128)} %top_hbm.1, ...), custom_call_target="tpu_custom_call" | custom-call | tf_op jit(solution)/shard_map/pallas_call | solution.py:406
  38.4 0.6 %copy.13 = f32[16,128]{1,0:T(8,128)} copy(f32[16,128]{1,0:T(8,128)S(1)} %get-tuple-element.6) | data formatting | bytes 16384
  39.0 0.6 %copy.14 = f32[16,128]{1,0:T(8,128)} copy(f32[16,128]{1,0:T(8,128)S(1)} %get-tuple-element.7) | data formatting | bytes 16384
  39.6 0.6 %copy.15 = f32[2,2,16]{2,1,0:T(2,128)} copy(f32[2,2,16]{2,1,0:T(2,128)S(1)} %get-tuple-element.8) | data formatting | bytes 512
Async XLA Ops:
  0.6 0.7 %copy-start = (f32[16]{0:T(128)S(1)}, f32[16]{0:T(128)}, u32[]{:S(2)}) copy-start(f32[16]{0:T(128)} %param.8) | copy-start | bytes 196
  0.6 0.7 %copy-start.1 = (f32[128]{0:T(128)S(1)}, f32[128]{0:T(128)}, u32[]{:S(2)}) copy-start(f32[128]{0:T(128)} %param.9) | copy-start | bytes 1540

commit v7 on v6

--- a/solution.py
+++ b/solution.py
@@ -396,7 +396,7 @@
 
 
 def on_device(n_row, n_col, points, inverse_length, target, probe_bits, leaf_inverse, top_basis, sub_basis):
-    low = math.gcd(n_col, 4)
+    low = math.gcd(n_col, 8)
     n_line, n_plane = low, n_row * (n_col // low)
     dim, own = points.shape
     cols = probe_bits.shape[0] + 1

time: 40.4 us -> 43.1 us (1.067)
  Pallas kernels: 37.1 us -> 39.8 us
    pallas_call x1, Pallas kernels: 37.1 us -> 39.8 us  [on_device(): pl.pallas_call(functools.partial(kernel, n_row, n_col, low, rank), out_sh...]
where the time goes in v7:
time: 43.1 us; the launch traced here: 42.9 us
  Pallas kernels  39.8 us (92%)
  local copies, waits for them, and re-layouts  2.43 us (6%)
  between operations  0.66 us (2%)
    pallas_call x1, Pallas kernels, on_device(): pl.pallas_call(functools.partial(kernel, n_row, n_col, low, rank), out_sh...  39.8 us
    unnamed x7, local copies, waits for them, and re-layouts  2.43 us

profile of v7, /device:TPU:0, one launch (start us, length us, event | category | flops | bytes accessed | tf_op | source)
XLA Modules:
  0.0 42.9 jit_solution(15628026302751983565)
XLA Ops:
  0.6 0.0 copy-start
  0.6 0.0 copy-start.1
  0.7 0.6 %copy-done = f32[16]{0:T(128)S(1)} copy-done((f32[16]{0:T(128)S(1)}, f32[16]{0:T(128)}, u32[]{:S(2)}) %copy-start) | copy-done | bytes 88
  1.3 0.0 copy-done.1
  1.3 39.8 %shard_map.94 = (f32[16,128]{1,0:T(8,128)S(1)}, f32[16,128]{1,0:T(8,128)S(1)}, f32[2,2,16]{2,1,0:T(2,128)S(1)}) custom-call(f32[16,128]{1,0:T(8,128)} %points_hbm.1, f32[1,16]{1,0:T(1,128)S(1)} %bitcast.2, f32[1,128]{1,0:T(1,128)S(1)} %bitcast.3, s32[15,128]{1,0:T(8,128)} %bits_hbm.1, f32[128,128]{1,0:T(8,128)} %leaf_hbm.1, f32[64,128]{1,0:T(8,128)} %top_hbm.1, ...), custom_call_target="tpu_custom_call" | custom-call | tf_op jit(solution)/shard_map/pallas_call | solution.py:406
  41.1 0.6 %copy.13 = f32[16,128]{1,0:T(8,128)} copy(f32[16,128]{1,0:T(8,128)S(1)} %get-tuple-element.6) | data formatting | bytes 16384
  41.7 0.6 %copy.14 = f32[16,128]{1,0:T(8,128)} copy(f32[16,128]{1,0:T(8,128)S(1)} %get-tuple-element.7) | data formatting | bytes 16384
  42.3 0.6 %copy.15 = f32[2,2,16]{2,1,0:T(2,128)} copy(f32[2,2,16]{2,1,0:T(2,128)S(1)} %get-tuple-element.8) | data formatting | bytes 512
Async XLA Ops:
  0.6 0.7 %copy-start = (f32[16]{0:T(128)S(1)}, f32[16]{0:T(128)}, u32[]{:S(2)}) copy-start(f32[16]{0:T(128)} %param.8) | copy-start | bytes 196
  0.6 0.7 %copy-start.1 = (f32[128]{0:T(128)S(1)}, f32[128]{0:T(128)}, u32[]{:S(2)}) copy-start(f32[128]{0:T(128)} %param.9) | copy-start | bytes 1540
